TPU v7x, 256 devices: a whole 4x4x8 slice. The times are simulated.
256 devices in a mesh: dp: 64 (over z, x, y_lo), tensor: 4 (over y_hi, core).
Axes of the slice: x: 4, y: 4 (y_hi: 2, y_lo: 2; y = y_hi * 2 + y_lo), z: 8, core: 2. Of those that a mesh axis runs over, the one named last changes fastest.
Arguments:
- tokens: bfloat16 [32768, 8192], P('dp'), may hold values from -6 to 6
- grad_out: bfloat16 [32768, 8192], P('dp', 'tensor'), may hold values from -0.015625 to 0.015625
- basis: bfloat16 [8192, 512], P(('dp', 'tensor')), may hold values from -0.5 to 0.5
- first_moment: float32 [512, 8192], P('dp', 'tensor'), may hold values from -0.3 to 0.3
- second_moment: float32 [512, 8192], P('dp', 'tensor'), may hold values from 0.02 to 0.2
Outputs:
- update: bfloat16 [8192, 8192], P('dp', 'tensor')
- new_first: float32 [512, 8192], P('dp', 'tensor')
- new_second: float32 [512, 8192], P('dp', 'tensor')
All inputs are finite; a program needn't handle non-finite values.
Results may differ from a plain program's by a relative error of at most 0.006.
Values may be sent and summed in bfloat16 or wider, within the bound.
No kernel may reach another device: no remote copies, remote signals or barrier semaphores. Data moves between devices by JAX's collectives and lax.ppermute only.
A program may use at most 64 MiB of HBM per device.

v0:
```python
import jax
import jax.numpy as jnp
from jax import lax
from jax.sharding import PartitionSpec as P

STEP = 20


def local(tokens, grad_out, basis, first_moment, second_moment):
    columns = tokens
    coords = jnp.dot(
        columns,
        lax.all_gather(basis, ("dp", "tensor"), axis=0, tiled=True),
        preferred_element_type=jnp.float32,
    )
    coords = coords.astype(jnp.bfloat16)
    columns = coords
    projected = lax.psum_scatter(
        lax.dot_general(
            columns, grad_out, (((0,), (0,)), ((), ())), preferred_element_type=jnp.float32
        ),
        "dp",
        scatter_dimension=0,
        tiled=True,
    )
    new_first = 0.9 * first_moment + 0.1 * projected
    new_second = 0.95 * second_moment + 0.05 * projected * projected
    first_fix = 1.0 - 0.9**STEP
    second_fix = 1.0 - 0.95**STEP
    step_dir = (new_first / first_fix / (jnp.sqrt(new_second / second_fix) + 1e-08)).astype(
        jnp.bfloat16
    )
    rows_here = lax.all_gather(basis, "tensor", axis=0, tiled=True)
    columns = rows_here
    update = jnp.dot(
        columns,
        lax.all_gather(step_dir, "dp", axis=0, tiled=True),
        preferred_element_type=jnp.float32,
    )
    return (update.astype(jnp.bfloat16), new_first, new_second)


def solution(mesh):
    placed = (
        P("dp", None),
        P("dp", "tensor"),
        P(("dp", "tensor"), None),
        P("dp", "tensor"),
        P("dp", "tensor"),
    )
    return jax.shard_map(
        local,
        mesh=mesh,
        in_specs=placed,
        out_specs=(P("dp", "tensor"), P("dp", "tensor"), P("dp", "tensor")),
        check_vma=False,
    )
```

profile of v0, /device:TPU:16, one launch (start us, length us, event | category | flops | bytes accessed | tf_op | source)
XLA Modules:
  0.0 1072.7 jit_solution(1138783851380941297)
XLA Ops:
  7.2 0.0 copy-start
  7.2 0.0 all-gather.3.cloned.1.call-start
  7.2 0.7 all-gather.3.cloned.1.call-update
  7.9 0.0 copy-start.2
  7.9 0.0 copy-start.3
  7.9 0.0 copy-start.1
  7.9 0.0 reduce-scatter.2.cloned.1.call-start
  8.0 420.7 %all-gather.3.cloned.1.call-done = bf16[8192,512]{1,0:T(8,128)(2,1)} async-done(((bf16[32,512]{1,0:T(8,128)(2,1)}), bf16[8192,512]{1,0:T(8,128)(2,1)}) %all-gather.3.cloned.1.call-update) | async-done | bytes 8388624 | tf_op jit(solution)/shard_map/all_gather | solution.py:13
  428.7 0.0 copy-done
  428.7 13.4 %fusion.1 = f32[512,2048]{1,0:T(8,128)} fusion(bf16[512,2048]{1,0:T(8,128)(2,1)S(1)} %copy-done, bf16[512,8192]{1,0:T(8,128)(2,1)} %param.5, bf16[8192,512]{1,0:T(8,128)(2,1)} %all-gather.3.cloned.1.call-done), kind=kOutput, calls=%fused_computation.3 | convolution fusion | flops 5368971264 | bytes 23068672 | tf_op jit(solution)/shard_map/dot_general | solution.py:19
  442.1 0.0 reduce-scatter.2.cloned.1.call-update
  442.1 0.0 all-gather.5.cloned.1.call-start
  442.2 322.9 %reduce-scatter.2.cloned.1.call-done = f32[8,2048]{1,0:T(8,128)} async-done(((f32[512,2048]{1,0:T(8,128)}), f32[8,2048]{1,0:T(8,128)}) %reduce-scatter.2.cloned.1.call-update) | async-done | bytes 65552 | tf_op jit(solution)/shard_map/reduce_scatter | solution.py:18
  765.0 0.0 copy-done.2
  765.0 0.0 copy-done.3
  765.0 1.5 divide_convert_fusion
  766.6 0.0 all-gather.5.cloned.1.call-update
  766.6 0.0 copy-done.1
  766.6 6.9 all_gather.11
  773.5 289.2 %all-gather.5.cloned.1.call-done = bf16[512,2048]{1,0:T(8,128)(2,1)} async-done(((bf16[8,2048]{1,0:T(8,128)(2,1)}), bf16[512,2048]{1,0:T(8,128)(2,1)}) %all-gather.5.cloned.1.call-update) | async-done | bytes 2097168 | tf_op jit(solution)/shard_map/all_gather | solution.py:37
  1062.8 2.3 fusion
  1065.1 1.0 copy.8
Async XLA Ops:
  7.2 421.5 %copy-start = (bf16[512,2048]{1,0:T(8,128)(2,1)S(1)}, bf16[512,2048]{1,0:T(8,128)(2,1)}, u32[]{:S(2)}) copy-start(bf16[512,2048]{1,0:T(8,128)(2,1)} %param.6) | copy-start | bytes 6291460
  7.2 421.5 %all-gather.3.cloned.1.call-start = ((), (), s32[]{:S(2)}) async-start(), calls=%async_computation.1 | async-start | bytes 8421376 | tf_op jit(solution)/shard_map/all_gather | solution.py:13
  7.9 757.1 %copy-start.2 = (f32[8,2048]{1,0:T(8,128)S(1)}, f32[8,2048]{1,0:T(8,128)}, u32[]{:S(2)}) copy-start(f32[8,2048]{1,0:T(8,128)} %param.8) | copy-start | bytes 196612
  7.9 757.1 %copy-start.3 = (f32[8,2048]{1,0:T(8,128)S(1)}, f32[8,2048]{1,0:T(8,128)}, u32[]{:S(2)}) copy-start(f32[8,2048]{1,0:T(8,128)} %param.9) | copy-start | bytes 196612
  7.9 758.7 %copy-start.1 = (bf16[32,512]{1,0:T(8,128)(2,1)S(1)}, bf16[32,512]{1,0:T(8,128)(2,1)}, u32[]{:S(2)}) copy-start(bf16[32,512]{1,0:T(8,128)(2,1)} %param.7) | copy-start | bytes 98308
  7.9 757.1 %reduce-scatter.2.cloned.1.call-start = ((), (), s32[]{:S(2)}) async-start(), calls=%async_computation.2 | async-start | bytes 4259840 | tf_op jit(solution)/shard_map/reduce_scatter | solution.py:18
  442.1 620.6 %all-gather.5.cloned.1.call-start = ((), (), s32[]{:S(2)}) async-start(), calls=%async_computation.3 | async-start | bytes 2129920 | tf_op jit(solution)/shard_map/all_gather | solution.py:37
Sparse Core Ops, SparseCore 0:
  9.9 418.7 all-gather.2
  442.2 322.7 reduce-scatter.1
  767.5 295.1 all-gather.4
where the time goes:
time: 1070 us
  waiting for transfers between devices  1030 us (96%)
  matrix products  15.8 us (1%)
  between operations  13.8 us (1%)
    all_gather x1, waiting for transfers between devices, local(): lax.all_gather(basis, ('dp', 'tensor'), axis=0, tiled=True)  421 us
    reduce_scatter x1, waiting for transfers between devices, local(): lax.psum_scatter(lax.dot_general(columns, grad_out, (((0,), (0,)), ((), (...  323 us
    all_gather x1, waiting for transfers between devices, local(): lax.all_gather(step_dir, 'dp', axis=0, tiled=True)  289 us
  transfers between devices with their start and end apart: 3, of which 3 were waited for; matrix products, arithmetic and copies ran while one was open for 0% of the time, Pallas kernels for 0%

commit v1 on v0

v1 whole, which is shorter than its diff:
```python
import jax
import jax.numpy as jnp
from jax import lax
from jax.sharding import Mesh, PartitionSpec as P

STEP = 20
AXES = ("z", "x", "yl", "yh", "core")
DP = ("z", "x", "yl")
TENSOR = ("yh", "core")
PLANE = ("x", "yl")
NZ, NX, NYL, NYH, NC = 8, 4, 2, 2, 2
NP = NX * NYL
NT = NYH * NC


def exchange(blocks, axes):
    return lax.all_to_all(blocks, axes, 0, 0, tiled=True)


def local(tokens, grad_out, basis, first_moment, second_moment):
    f32, bf16 = jnp.float32, jnp.bfloat16
    rows, rank = basis.shape
    quarter = rank // NT
    dim = tokens.shape[1]
    columns = grad_out.shape[1]
    own = rank // (NZ * NP)

    pieces = basis.reshape(rows, NT, quarter).transpose(1, 0, 2)
    pieces = jnp.broadcast_to(pieces[None], (NZ, NT, rows, quarter))
    line = exchange(pieces.reshape(NZ * NT, rows, quarter), ("z",) + TENSOR)
    plane = exchange(jnp.broadcast_to(line[None], (NP,) + line.shape), PLANE)
    basis_part = plane.reshape(NP, NZ, NT * rows, quarter).transpose(1, 0, 2, 3).reshape(dim, quarter)

    coords = jnp.dot(tokens, basis_part, preferred_element_type=f32).astype(bf16)
    coords = lax.all_gather(coords.T, TENSOR, axis=0, tiled=True)

    coords = coords.reshape(NZ, NP, own, -1).transpose(1, 0, 2, 3).reshape(rank, -1)
    partial = jnp.dot(coords, grad_out, preferred_element_type=f32).astype(bf16)
    partial = exchange(partial.reshape(NP, NZ * own, columns), PLANE)
    partial = jnp.sum(partial.astype(f32), axis=0).astype(bf16)
    partial = exchange(partial.reshape(NZ, own, columns), ("z",))
    projected = jnp.sum(partial.astype(f32), axis=0)

    new_first = 0.9 * first_moment + 0.1 * projected
    new_second = 0.95 * second_moment + 0.05 * projected * projected
    first_fix = 1.0 - 0.9**STEP
    second_fix = 1.0 - 0.95**STEP
    step_dir = (new_first / first_fix / (jnp.sqrt(new_second / second_fix) + 1e-08)).astype(bf16)

    line = exchange(jnp.broadcast_to(step_dir[None], (NZ, own, columns)), ("z",))
    plane = exchange(jnp.broadcast_to(line[None], (NP,) + line.shape), PLANE)
    rows_here = lax.all_gather(basis, TENSOR, axis=0, tiled=True)
    rows_here = rows_here.reshape(-1, NZ, NP, own).transpose(0, 2, 1, 3).reshape(-1, rank)
    update = jnp.dot(rows_here, plane.reshape(rank, columns), preferred_element_type=f32)
    return (update.astype(bf16), new_first, new_second)


def solution(mesh):
    fine = Mesh(mesh.devices.reshape(NZ, NX, NYL, NYH, NC), AXES)
    placed = (
        P(DP, None),
        P(DP, TENSOR),
        P(DP + TENSOR, None),
        P(DP, TENSOR),
        P(DP, TENSOR),
    )
    return jax.shard_map(
        local,
        mesh=fine,
        in_specs=placed,
        out_specs=(P(DP, TENSOR), P(DP, TENSOR), P(DP, TENSOR)),
        check_vma=False,
    )
```

time: 1070 us -> 167 us (0.16)
  waiting for transfers between devices: 1030 us -> 4.95 us
  blocking collectives: 6.93 us -> 142 us
  between operations: 13.8 us -> 0.77 us
    all_gather x2 -> x0, waiting for transfers between devices: 710 us -> none  [the longest x1 421 us: local(): lax.all_gather(basis, ('dp', 'tensor'), axis=0, tiled=True)]
    reduce_scatter x1 -> x0, waiting for transfers between devices: 323 us -> none  [local(): lax.psum_scatter(lax.dot_general(columns, grad_out, (((0,), (0,)), ((), (...]
    all_to_all x0 -> x5, blocking collectives: none -> 112 us  [exchange(): return lax.all_to_all(blocks, axes, 0, 0, tiled=True)]
    all_gather x1 -> x2, blocking collectives: 6.93 us -> 30.1 us  [the longest x1 22 us: local(): rows_here = lax.all_gather(basis, TENSOR, axis=0, tiled=True)]
  transfers between devices with their start and end apart: 3 -> 1, of which waited for: 3 -> 1; matrix products, arithmetic and copies ran while one was open for 0% -> 0% of each run, Pallas kernels for 0% -> 0%
where the time goes in v1:
time: 167 us; the launch traced here: 166 us
  blocking collectives  142 us (85%)
  matrix products  6.68 us (4%)
  waiting for transfers between devices  4.95 us (3%)
  starting transfers between devices  4.46 us (3%)
  local copies, waits for them, and re-layouts  4.22 us (3%)
  other arithmetic  2.73 us (2%)
    all_to_all x5, blocking collectives, exchange(): return lax.all_to_all(blocks, axes, 0, 0, tiled=True)  112 us
    all_gather x1, blocking collectives, local(): rows_here = lax.all_gather(basis, TENSOR, axis=0, tiled=True)  22 us
    all_gather x1, blocking collectives, local(): coords = lax.all_gather(coords.T, TENSOR, axis=0, tiled=True)  8.02 us
    all_to_all x1, waiting for transfers between devices, exchange(): return lax.all_to_all(blocks, axes, 0, 0, tiled=True)  4.95 us
    all_to_all x1, starting transfers between devices, exchange(): return lax.all_to_all(blocks, axes, 0, 0, tiled=True)  4.46 us
  transfers between devices with their start and end apart: 1, of which 1 were waited for; matrix products, arithmetic and copies ran while one was open for 0% of the time, Pallas kernels for 0%

profile of v1, /device:TPU:16, one launch (start us, length us, event | category | flops | bytes accessed | tf_op | source)
XLA Modules:
  0.0 166.1 jit_solution(3452379733097423211)
XLA Ops:
  0.6 0.0 copy-start
  0.6 0.9 reshape.39
  1.6 23.5 %all_to_all.30 = bf16[32,32,128]{2,1,0:T(8,128)(2,1)S(1)} all-to-all(bf16[32,32,128]{2,1,0:T(8,128)(2,1)S(1)} %bitcast.36), channel_id=1, replica_groups=mesh['z'=8,'x'=4,'yl'=2,'yh'=2,'core'=2] {'z','yh','core'}, dimensions={0} | all-to-all | bytes 524288 | tf_op jit(solution)/shard_map/all_to_all | solution.py:17
  25.1 0.3 broadcast_in_dim.9
  25.5 0.0 copy-start.1
  25.5 31.1 %all_to_all.31 = bf16[8,32,32,128]{3,2,1,0:T(8,128)(2,1)S(1)} all-to-all(bf16[8,32,32,128]{3,2,1,0:T(8,128)(2,1)S(1)} %broadcast_in_dim.9), channel_id=1, replica_groups=mesh['z'=8,'x'=4,'yl'=2,'yh'=2,'core'=2] {'x','yl'}, dimensions={0} | all-to-all | bytes 4194304 | tf_op jit(solution)/shard_map/all_to_all | solution.py:17
  56.6 0.1 copy.28
  56.8 0.0 copy-done.1
  56.8 2.9 %convolution_convert_fusion.1 = bf16[128,512]{1,0:T(8,128)(2,1)S(1)} fusion(bf16[8192,128]{1,0:T(8,128)(2,1)S(1)} %bitcast.32, bf16[512,8192]{1,0:T(8,128)(2,1)S(1)} %copy-done.1), kind=kOutput, calls=%fused_computation.4 | convolution fusion | flops 1073807360 | bytes 10616832 | tf_op jit(solution)/shard_map/dot_general | solution.py:34
  59.7 8.0 %all_gather.6 = bf16[512,512]{1,0:T(8,128)(2,1)S(1)} all-gather(bf16[128,512]{1,0:T(8,128)(2,1)S(1)} %convolution_convert_fusion.1), channel_id=1, replica_groups=mesh['z'=8,'x'=4,'yl'=2,'yh'=2,'core'=2] {'yh','core'}, dimensions={0}, use_global_device_ids=true | all-gather | bytes 655360 | tf_op jit(solution)/shard_map/all_gather | solution.py:35
  67.7 0.0 copy-done
  67.7 1.3 convolution_convert_fusion
  69.0 30.5 %all_to_all.32 = bf16[8,64,2048]{2,1,0:T(8,128)(2,1)} all-to-all(bf16[8,64,2048]{2,1,0:T(8,128)(2,1)S(1)} %bitcast.34), channel_id=1, replica_groups=mesh['z'=8,'x'=4,'yl'=2,'yh'=2,'core'=2] {'x','yl'}, dimensions={0} | all-to-all | bytes 4194304 | tf_op jit(solution)/shard_map/all_to_all | solution.py:17
  99.5 0.0 copy-start.3
  99.5 0.0 copy-start.4
  99.5 2.0 %reduce_sum.21 = bf16[64,2048]{1,0:T(8,128)(2,1)S(1)} reduce(bf16[8,64,2048]{2,1,0:T(8,128)(2,1)} %all_to_all.32, bf16[]{:T(256)} %constant.4.clone.1), dimensions={0}, to_apply=%region_0.0 | reduce | flops 917504 | bytes 2359298 | tf_op jit(solution)/shard_map/reduce_sum | solution.py:40
  101.5 14.2 %all_to_all.33 = bf16[8,8,2048]{2,1,0:T(8,128)(2,1)S(1)} all-to-all(bf16[8,8,2048]{2,1,0:T(8,128)(2,1)S(1)} %bitcast.35), channel_id=1, replica_groups=mesh['z'=8,'x'=4,'yl'=2,'yh'=2,'core'=2] {'z'}, dimensions={0} | all-to-all | bytes 524288 | tf_op jit(solution)/shard_map/all_to_all | solution.py:17
  115.7 0.0 copy-done.3
  115.8 0.0 copy-done.4
  115.8 0.7 divide_convert_fusion
  116.5 12.9 %all_to_all.34 = bf16[8,8,2048]{2,1,0:T(8,128)(2,1)S(1)} all-to-all(bf16[8,8,2048]{2,1,0:T(8,128)(2,1)S(1)} %broadcast_in_dim.10), channel_id=1, replica_groups=mesh['z'=8,'x'=4,'yl'=2,'yh'=2,'core'=2] {'z'}, dimensions={0} | all-to-all | bytes 524288 | tf_op jit(solution)/shard_map/all_to_all | solution.py:17
  129.4 1.6 broadcast_in_dim.11
  130.9 0.0 copy-start.2
  130.9 4.5 %all-to-all-start.5 = ((bf16[8,8,8,2048]{3,2,1,0:T(8,128)(2,1)}), bf16[8,8,8,2048]{3,2,1,0:T(8,128)(2,1)}, u32[]{:S(2)}, u32[]{:S(2)}) async-start(bf16[8,8,8,2048]{3,2,1,0:T(8,128)(2,1)} %broadcast_in_dim.11), calls=%async_computation.5 | async-start | bytes 4194304 | tf_op jit(solution)/shard_map/all_to_all | solution.py:17
  135.4 0.0 copy-done.2
  135.4 22.0 %all_gather.7 = bf16[128,512]{1,0:T(8,128)(2,1)S(1)} all-gather(bf16[32,512]{1,0:T(8,128)(2,1)S(1)} %copy-done.2), channel_id=1, replica_groups=mesh['z'=8,'x'=4,'yl'=2,'yh'=2,'core'=2] {'yh','core'}, dimensions={0}, use_global_device_ids=true | all-gather | bytes 163840 | tf_op jit(solution)/shard_map/all_gather | solution.py:52
  157.5 0.1 copy.30
  157.6 5.0 %all-to-all-done.5 = bf16[8,8,8,2048]{3,2,1,0:T(8,128)(2,1)} async-done(((bf16[8,8,8,2048]{3,2,1,0:T(8,128)(2,1)}), bf16[8,8,8,2048]{3,2,1,0:T(8,128)(2,1)}, u32[]{:S(2)}, u32[]{:S(2)}) %all-to-all-start.5) | async-done | bytes 2097184 | tf_op jit(solution)/shard_map/all_to_all | solution.py:17
  162.5 2.5 %fusion.1 = bf16[128,2048]{0,1:T(8,128)(2,1)S(1)} fusion(bf16[8,8,8,2048]{3,2,1,0:T(8,128)(2,1)} %all-to-all-done.5, bf16[128,8,8,8]{0,3,2,1:T(8,128)(2,1)S(1)} %bitcast.38), kind=kOutput, calls=%fused_computation.3 | convolution fusion | flops 268697600 | bytes 2752512 | tf_op jit(solution)/shard_map/dot_general | solution.py:54
  165.1 1.0 copy.32
  (5 shorter events, 0.1 us)
Async XLA Ops:
  0.6 67.1 %copy-start = (bf16[512,2048]{1,0:T(8,128)(2,1)S(1)}, bf16[512,2048]{1,0:T(8,128)(2,1)}, u32[]{:S(2)}) copy-start(bf16[512,2048]{1,0:T(8,128)(2,1)} %param.6) | copy-start | bytes 6291460
  25.5 31.3 %copy-start.1 = (bf16[512,8192]{1,0:T(8,128)(2,1)S(1)}, bf16[512,8192]{1,0:T(8,128)(2,1)}, u32[]{:S(2)}) copy-start(bf16[512,8192]{1,0:T(8,128)(2,1)} %param.5) | copy-start | bytes 25165828
  99.5 16.3 %copy-start.3 = (f32[8,2048]{1,0:T(8,128)S(1)}, f32[8,2048]{1,0:T(8,128)}, u32[]{:S(2)}) copy-start(f32[8,2048]{1,0:T(8,128)} %param.8) | copy-start | bytes 196612
  99.5 16.3 %copy-start.4 = (f32[8,2048]{1,0:T(8,128)S(1)}, f32[8,2048]{1,0:T(8,128)}, u32[]{:S(2)}) copy-start(f32[8,2048]{1,0:T(8,128)} %param.9) | copy-start | bytes 196612
  130.9 4.5 %copy-start.2 = (bf16[32,512]{1,0:T(8,128)(2,1)S(1)}, bf16[32,512]{1,0:T(8,128)(2,1)}, u32[]{:S(2)}) copy-start(bf16[32,512]{1,0:T(8,128)(2,1)} %param.7) | copy-start | bytes 98308
  130.9 31.6 %all-to-all-start.5 = ((bf16[8,8,8,2048]{3,2,1,0:T(8,128)(2,1)}), bf16[8,8,8,2048]{3,2,1,0:T(8,128)(2,1)}, u32[]{:S(2)}, u32[]{:S(2)}) async-start(bf16[8,8,8,2048]{3,2,1,0:T(8,128)(2,1)} %broadcast_in_dim.11), calls=%async_computation.5 | async-start | bytes 4194304 | tf_op jit(solution)/shard_map/all_to_all | solution.py:17

commit v2 on v1

v2 whole, which is shorter than its diff:
```python
import jax
import jax.numpy as jnp
from jax import lax
from jax.experimental import pallas as pl
from jax.experimental.pallas import tpu as pltpu
from jax.sharding import Mesh, PartitionSpec as P

STEP = 20
AXES = ("z", "x", "yl", "yh", "core")
DP = ("z", "x", "yl")
TENSOR = ("yh", "core")
PLANE = ("x", "yl")
NZ, NX, NYL, NYH, NC = 8, 4, 2, 2, 2
NP = NX * NYL
NT = NYH * NC
MIB = 1024 * 1024
F32, BF16 = jnp.float32, jnp.bfloat16


def exchange(blocks, axes):
    return lax.all_to_all(blocks, axes, 0, 0, tiled=True)


def gather(block, axes, members):
    return exchange(jnp.broadcast_to(block[None], (members,) + block.shape), axes)


def swap(block, axis):
    return lax.ppermute(block, axis, ((0, 1), (1, 0)))


def peers(block):
    far = swap(block, "yh")
    return block, swap(block, "core"), far, swap(far, "core")


def halves(value):
    high = value.astype(BF16)
    return high, (value - high.astype(F32)).astype(BF16)


def call(kernel, index, grid, in_specs, out_specs, out_shape, scratch, cost, limit, *args):
    return pl.pallas_call(
        kernel,
        grid_spec=pltpu.PrefetchScalarGridSpec(
            num_scalar_prefetch=1,
            grid=grid,
            in_specs=in_specs,
            out_specs=out_specs,
            scratch_shapes=scratch,
        ),
        out_shape=out_shape,
        compiler_params=pltpu.CompilerParams(vmem_limit_bytes=limit * MIB),
        cost_estimate=pl.CostEstimate(flops=cost[0], bytes_accessed=cost[1], transcendentals=0),
    )(index, *args)


def quarter_copies(index, pieces):
    rows, rank = pieces[0].shape
    quarter = rank // NT
    group = NT * rows

    def kernel(index_ref, *refs):
        out = refs[-1]
        for k in range(NT):
            start = pl.multiple_of((index_ref[0] ^ k) * rows, rows)
            for z in range(NZ):
                out[z, pl.ds(start, rows), :] = refs[k][...]

    return call(
        kernel,
        index,
        (1,),
        [pl.BlockSpec((rows, quarter), lambda i, t: (0, t[0]))] * NT,
        pl.BlockSpec((NZ, group, quarter), lambda i, t: (0, 0, 0)),
        jax.ShapeDtypeStruct((NZ, group, quarter), BF16),
        [],
        (0, 2 * NZ * group * quarter),
        16,
        *pieces,
    )


def coordinates(tokens, plane):
    part = plane.transpose(1, 0, 2, 3).reshape(tokens.shape[1], plane.shape[3])
    return jnp.dot(tokens, part, preferred_element_type=F32).astype(BF16).T


def partial_sums(index, coords, grad_out, first_moment, second_moment):
    quarter, count = coords[0].shape
    rank, columns = NT * quarter, grad_out.shape[1]
    own, part = first_moment.shape[0], columns // NP
    rows = rank + 4 * own

    def kernel(index_ref, *refs):
        pieces, (grad_ref, first_ref, second_ref, out) = refs[:NT], refs[NT:]
        for k in range(NT):
            start = pl.multiple_of((index_ref[0] ^ k) * quarter, quarter)
            out[0, pl.ds(start, quarter), :] = jnp.dot(
                pieces[k][...], grad_ref[...], preferred_element_type=F32
            ).astype(BF16)
        out[0, rank : rank + 2 * own, :] = jnp.concatenate(halves(first_ref[...]))
        out[0, rank + 2 * own :, :] = jnp.concatenate(halves(second_ref[...]))

    return call(
        kernel,
        index,
        (NP,),
        [pl.BlockSpec((quarter, count), lambda p, t: (0, 0))] * NT
        + [pl.BlockSpec((count, part), lambda p, t: (0, p))]
        + [pl.BlockSpec((own, part), lambda p, t: (0, p))] * 2,
        pl.BlockSpec((1, rows, part), lambda p, t: (p, 0, 0)),
        jax.ShapeDtypeStruct((NP, rows, part), BF16),
        [],
        (2 * rank * count * columns, 2 * columns * (count + rows)),
        24,
        *coords,
        grad_out,
        first_moment,
        second_moment,
    )


def plane_sums(index, received, own):
    members, rows, part = received.shape
    rank = rows - 4 * own
    step = rank // 4

    def kernel(index_ref, sums_ref, moments_ref, out, first, second):
        total = sums_ref[0].astype(F32)
        for source in range(1, members):
            total += sums_ref[source].astype(F32)
        out[...] = total.astype(BF16)

        @pl.when(pl.program_id(0) == 0)
        def _():
            for source in range(members):
                block = moments_ref[source].astype(F32)
                here = slice(source * own, (source + 1) * own)
                first[here, :] = block[:own] + block[own : 2 * own]
                second[here, :] = block[2 * own : 3 * own] + block[3 * own :]

    return call(
        kernel,
        index,
        (4,),
        [
            pl.BlockSpec((members, step, part), lambda i, t: (0, i, 0)),
            pl.BlockSpec((members, 4 * own, part), lambda i, t: (0, rank // (4 * own), 0)),
        ],
        [
            pl.BlockSpec((step, part), lambda i, t: (i, 0)),
            pl.BlockSpec((members * own, part), lambda i, t: (0, 0)),
            pl.BlockSpec((members * own, part), lambda i, t: (0, 0)),
        ],
        [
            jax.ShapeDtypeStruct((rank, part), BF16),
            jax.ShapeDtypeStruct((members * own, part), F32),
            jax.ShapeDtypeStruct((members * own, part), F32),
        ],
        [],
        (members * rank * part, 2 * members * rows * part),
        24,
        received,
        received,
    )


def update_blocks(index, pieces, step_dir, projected, own):
    quarter = pieces[0].shape[1]
    group = pieces[0].shape[0] // NP
    part = step_dir.shape[1]

    def kernel(index_ref, *refs):
        blocks, (step_ref, projected_ref, out) = refs[:NT], refs[NT:]
        total = 0.0
        for k in range(NT):
            start = pl.multiple_of((index_ref[0] ^ k) * quarter, quarter)
            total += jnp.dot(
                blocks[k][...], step_ref[pl.ds(start, quarter), :], preferred_element_type=F32
            )
        out[0, :group, :] = total.astype(BF16)
        out[0, group:, :] = jnp.concatenate(halves(projected_ref[...]))

    return call(
        kernel,
        index,
        (NP,),
        [pl.BlockSpec((group, quarter), lambda p, t: (p, 0))] * NT
        + [
            pl.BlockSpec((NT * quarter, part), lambda p, t: (0, 0)),
            pl.BlockSpec((own, part), lambda p, t: (p, 0)),
        ],
        pl.BlockSpec((1, group + 2 * own, part), lambda p, t: (p, 0, 0)),
        jax.ShapeDtypeStruct((NP, group + 2 * own, part), BF16),
        [],
        (2 * NP * group * NT * quarter * part, 2 * NP * group * (NT * quarter + part)),
        24,
        *pieces,
        step_dir,
        projected,
    )


def moments_of(first_moment, second_moment, projected):
    new_first = 0.9 * first_moment + 0.1 * projected
    new_second = 0.95 * second_moment + 0.05 * projected * projected
    return new_first, new_second


def local(tokens, grad_out, basis, first_moment, second_moment):
    rows, rank = basis.shape
    quarter = rank // NT
    group = NT * rows
    columns = grad_out.shape[1]
    own = rank // (NZ * NP)
    part = columns // NP
    index = (NC * lax.axis_index("yh") + lax.axis_index("core")).astype(jnp.int32).reshape(1)

    line = exchange(quarter_copies(index, peers(basis)), ("z",))
    plane = gather(line, PLANE, NP)
    coords = peers(coordinates(tokens, plane))

    partial = partial_sums(index, coords, grad_out, first_moment, second_moment)
    partial, first_part, second_part = plane_sums(index, exchange(partial, PLANE), own)

    plane, partial = lax.optimization_barrier((plane, partial))
    rows_here = lax.dynamic_index_in_dim(plane, lax.axis_index("z"), axis=1, keepdims=False)
    rows_here = peers(rows_here.reshape(NP * group, quarter))

    partial = exchange(partial.reshape(NZ, NP * own, part), ("z",))
    projected = jnp.sum(partial.astype(F32), axis=0)
    new_first, new_second = moments_of(first_part, second_part, projected)
    first_fix = 1.0 - 0.9**STEP
    second_fix = 1.0 - 0.95**STEP
    step_dir = (new_first / first_fix / (jnp.sqrt(new_second / second_fix) + 1e-08)).astype(BF16)
    step_dir = gather(step_dir, ("z",), NZ).reshape(rank, part)

    back = update_blocks(index, rows_here, step_dir, projected, own)
    back = exchange(back, PLANE).transpose(1, 0, 2).reshape(group + 2 * own, columns)
    projected = back[group : group + own].astype(F32) + back[group + own :].astype(F32)
    new_first, new_second = moments_of(first_moment, second_moment, projected)
    return (back[:group], new_first, new_second)


def solution(mesh):
    fine = Mesh(mesh.devices.reshape(NZ, NX, NYL, NYH, NC), AXES)
    placed = (
        P(DP, None),
        P(DP, TENSOR),
        P(DP + TENSOR, None),
        P(DP, TENSOR),
        P(DP, TENSOR),
    )
    return jax.shard_map(
        local,
        mesh=fine,
        in_specs=placed,
        out_specs=(P(DP, TENSOR), P(DP, TENSOR), P(DP, TENSOR)),
        check_vma=False,
    )
```

time: 167 us -> 152 us (0.910)
  blocking collectives: 142 us -> 94.9 us
  waiting for transfers between devices: 4.95 us -> 31.5 us
  starting transfers between devices: 4.46 us -> 11 us
  Pallas kernels: 0 us -> 6.4 us
  matrix products: 6.68 us -> 2.91 us
  other arithmetic: 2.73 us -> 0.78 us
    all_gather x2 -> x0, blocking collectives: 30.1 us -> none  [the longest x1 22 us: local(): rows_here = lax.all_gather(basis, TENSOR, axis=0, tiled=True)]
    all_to_all x5 -> x4, blocking collectives: 112 us -> 94.9 us  [exchange(): return lax.all_to_all(blocks, axes, 0, 0, tiled=True)]
    ppermute x0 -> x9, waiting for transfers between devices: none -> 13.3 us  [swap(): return lax.ppermute(block, axis, ((0, 1), (1, 0)))]
    all_to_all x1 -> x2, waiting for transfers between devices: 4.95 us -> 18.2 us  [exchange(): return lax.all_to_all(blocks, axes, 0, 0, tiled=True)]
    pallas_call x0 -> x4, Pallas kernels: none -> 6.4 us  [call(): pl.pallas_call(kernel, grid_spec=pltpu.PrefetchScalarGridSpec(num_scalar_...]
    ppermute x0 -> x9, starting transfers between devices: none -> 4.18 us  [swap(): return lax.ppermute(block, axis, ((0, 1), (1, 0)))]
    dot_general x3 -> x1, matrix products: 6.68 us -> 2.91 us  [coordinates(): return jnp.dot(tokens, part, preferred_element_type=F32).astype(BF16).T]
    all_to_all x1 -> x2, starting transfers between devices: 4.46 us -> 6.83 us  [exchange(): return lax.all_to_all(blocks, axes, 0, 0, tiled=True)]
  transfers between devices with their start and end apart: 1 -> 11, of which waited for: 1 -> 8; matrix products, arithmetic and copies ran while one was open for 0% -> 1% of each run, Pallas kernels for 0% -> 0%
where the time goes in v2:
time: 152 us
  blocking collectives  94.9 us (62%)
  waiting for transfers between devices  31.5 us (21%)
  starting transfers between devices  11 us (7%)
  Pallas kernels  6.4 us (4%)
  local copies, waits for them, and re-layouts  3.58 us (2%)
  matrix products  2.91 us (2%)
    all_to_all x4, blocking collectives, exchange(): return lax.all_to_all(blocks, axes, 0, 0, tiled=True)  94.9 us
    all_to_all x2, waiting for transfers between devices, exchange(): return lax.all_to_all(blocks, axes, 0, 0, tiled=True)  18.2 us
    ppermute x9, waiting for transfers between devices, swap(): return lax.ppermute(block, axis, ((0, 1), (1, 0)))  13.3 us
    all_to_all x2, starting transfers between devices, exchange(): return lax.all_to_all(blocks, axes, 0, 0, tiled=True)  6.83 us
    pallas_call x4, Pallas kernels, call(): pl.pallas_call(kernel, grid_spec=pltpu.PrefetchScalarGridSpec(num_scalar_...  6.4 us
    ppermute x9, starting transfers between devices, swap(): return lax.ppermute(block, axis, ((0, 1), (1, 0)))  4.18 us
  transfers between devices with their start and end apart: 11, of which 8 were waited for; matrix products, arithmetic and copies ran while one was open for 1% of the time, Pallas kernels for 0%

profile of v2, /device:TPU:16, one launch (start us, length us, event | category | flops | bytes accessed | tf_op | source)
XLA Modules:
  0.0 152.0 jit_solution(8885704394482820992)
XLA Ops:
  0.6 2.2 %collective-permute-start.1 = (bf16[32,512]{1,0:T(8,128)(2,1)}, bf16[32,512]{1,0:T(8,128)(2,1)S(1)}, u32[]{:S(2)}, u32[]{:S(2)}) collective-permute-start(bf16[32,512]{1,0:T(8,128)(2,1)} %refs_0_.1), channel_id=1, source_target_pairs={{0,2},{2,0},{1,3},{3,1},{4,6},{6,4},{5,7},{7,5},{8,10},{10,8},{9,1... | collective-permute-start | bytes 98312 | tf_op jit(solution)/shard_map/ppermute | solution.py:29
  2.8 0.0 collective-permute-start
  2.8 3.6 %collective-permute-done.1.refs_2_ = bf16[32,512]{1,0:T(8,128)(2,1)S(1)} collective-permute-done((bf16[32,512]{1,0:T(8,128)(2,1)}, bf16[32,512]{1,0:T(8,128)(2,1)S(1)}, u32[]{:S(2)}, u32[]{:S(2)}) %collective-permute-start.1) | collective-permute-done | bytes 32800 | tf_op jit(solution)/shard_map/ppermute | solution.py:29
  6.3 0.0 collective-permute-start.2
  6.3 0.0 collective-permute-done.refs_1_
  6.4 1.2 collective-permute-done.2.refs_3_
  7.6 0.0 copy-start.3
  7.6 0.8 copy-done.3
  8.4 20.5 %all_to_all.30 = bf16[8,128,128]{2,1,0:T(8,128)(2,1)S(1)} all-to-all(bf16[8,128,128]{2,1,0:T(8,128)(2,1)S(1)} %shard_map.76), channel_id=1, replica_groups=mesh['z'=8,'x'=4,'yl'=2,'yh'=2,'core'=2] {'z'}, dimensions={0} | all-to-all | bytes 524288 | tf_op jit(solution)/shard_map/all_to_all | solution.py:21
  28.8 0.5 broadcast_in_dim.4
  29.3 0.0 copy-start.4
  29.3 30.7 %all_to_all.31 = bf16[8,8,128,128]{3,2,1,0:T(8,128)(2,1)S(1)} all-to-all(bf16[8,8,128,128]{3,2,1,0:T(8,128)(2,1)S(1)} %broadcast_in_dim.4), channel_id=1, replica_groups=mesh['z'=8,'x'=4,'yl'=2,'yh'=2,'core'=2] {'x','yl'}, dimensions={0} | all-to-all | bytes 4194304 | tf_op jit(solution)/shard_map/all_to_all | solution.py:21
  60.0 0.2 copy.12
  60.3 0.0 copy-done.4
  60.3 0.0 copy-start
  60.3 0.0 copy-start.1
  60.3 0.0 copy-start.2
  60.3 2.9 %convolution_convert_fusion.refs_0_ = bf16[128,512]{1,0:T(8,128)(2,1)S(1)} fusion(bf16[8192,128]{1,0:T(8,128)(2,1)S(1)} %bitcast.16, bf16[512,8192]{1,0:T(8,128)(2,1)S(1)} %copy-done.4), kind=kOutput, calls=%fused_computation | convolution fusion | flops 1073807360 | bytes 10616832 | tf_op jit(solution)/shard_map/dot_general | solution.py:86
  63.2 0.7 collective-permute-start.4
  64.0 0.0 collective-permute-start.3
  64.0 5.8 %collective-permute-done.4.refs_2_ = bf16[128,512]{1,0:T(8,128)(2,1)S(1)} collective-permute-done((bf16[128,512]{1,0:T(8,128)(2,1)S(1)}, bf16[128,512]{1,0:T(8,128)(2,1)S(1)}, u32[]{:S(2)}, u32[]{:S(2)}) %collective-permute-start.4) | collective-permute-done | bytes 131104 | tf_op jit(solution)/shard_map/ppermute | solution.py:29
  69.8 0.0 collective-permute-start.5
  69.8 0.0 collective-permute-done.3.refs_1_
  69.8 1.3 collective-permute-done.5.refs_3_
  71.1 0.0 copy-done
  71.2 0.0 copy-done.1
  71.2 0.0 copy-done.2
  71.2 2.9 %shard_map.77 = bf16[8,544,256]{2,1,0:T(8,128)(2,1)S(1)} custom-call(s32[1]{0:T(128)} %bitcast.index_ref, bf16[128,512]{1,0:T(8,128)(2,1)S(1)} %convolution_convert_fusion.refs_0_, bf16[128,512]{1,0:T(8,128)(2,1)S(1)} %collective-permute-done.3.refs_1_, bf16[128,512]{1,0:T(8,128)(2,1)S(1)} %collective-permute-done.4.refs_2_, ...), custom_call_target="tpu_custom_call" | custom-call | flops 1073741824 | bytes 4325376 | tf_op jit(solution)/shard_map/pallas_call | solution.py:43
  74.1 31.3 %all_to_all.32.sums_ref.moments_ref = bf16[8,544,256]{2,1,0:T(8,128)(2,1)S(1)} all-to-all(bf16[8,544,256]{2,1,0:T(8,128)(2,1)S(1)} %shard_map.77), channel_id=1, replica_groups=mesh['z'=8,'x'=4,'yl'=2,'yh'=2,'core'=2] {'x','yl'}, dimensions={0} | all-to-all | bytes 4456448 | tf_op jit(solution)/shard_map/all_to_all | solution.py:21
  105.4 1.7 %shard_map.78 = (bf16[512,256]{1,0:T(8,128)(2,1)}, f32[64,256]{1,0:T(8,128)S(1)}, f32[64,256]{1,0:T(8,128)S(1)}) custom-call(s32[1]{0:T(128)} %bitcast.index_ref, bf16[8,544,256]{2,1,0:T(8,128)(2,1)S(1)} %all_to_all.32.sums_ref.moments_ref, bf16[8,544,256]{2,1,0:T(8,128)(2,1)S(1)} %all_to_all.32.sums_ref.moments_ref), custom_call_target="tpu_custom_call" | custom-call | flops 1048576 | bytes 2228224 | tf_op jit(solution)/shard_map/pallas_call | solution.py:43
  107.1 3.4 %all-to-all-start.3 = ((bf16[8,64,256]{2,1,0:T(8,128)(2,1)}), bf16[8,64,256]{2,1,0:T(8,128)(2,1)S(1)}, u32[]{:S(2)}, u32[]{:S(2)}) async-start(bf16[8,64,256]{2,1,0:T(8,128)(2,1)} %bitcast.4), calls=%async_computation.3 | async-start | bytes 524288 | tf_op jit(solution)/shard_map/all_to_all | solution.py:21
  110.5 0.7 collective-permute-start.7
  111.3 9.8 %all-to-all-done.3 = bf16[8,64,256]{2,1,0:T(8,128)(2,1)S(1)} async-done(((bf16[8,64,256]{2,1,0:T(8,128)(2,1)}), bf16[8,64,256]{2,1,0:T(8,128)(2,1)S(1)}, u32[]{:S(2)}, u32[]{:S(2)}) %all-to-all-start.3) | async-done | bytes 262176 | tf_op jit(solution)/shard_map/all_to_all | solution.py:21
  121.1 0.1 fusion.6
  121.2 0.7 broadcast_in_dim.5
  121.9 3.4 %all-to-all-start.4 = ((bf16[8,64,256]{2,1,0:T(8,128)(2,1)}), bf16[8,64,256]{2,1,0:T(8,128)(2,1)S(1)}, u32[]{:S(2)}, u32[]{:S(2)}) async-start(bf16[8,64,256]{2,1,0:T(8,128)(2,1)} %broadcast_in_dim.5), calls=%async_computation.4 | async-start | bytes 524288 | tf_op jit(solution)/shard_map/all_to_all | solution.py:21
  125.3 0.1 collective-permute-start.6
  125.4 0.0 collective-permute-done.7.refs_2_
  125.4 0.5 collective-permute-start.8
  125.9 1.0 collective-permute-done.6.refs_1_
  126.9 0.4 collective-permute-done.8.refs_3_
  127.3 8.4 %all-to-all-done.4 = bf16[8,64,256]{2,1,0:T(8,128)(2,1)S(1)} async-done(((bf16[8,64,256]{2,1,0:T(8,128)(2,1)}), bf16[8,64,256]{2,1,0:T(8,128)(2,1)S(1)}, u32[]{:S(2)}, u32[]{:S(2)}) %all-to-all-start.4) | async-done | bytes 262176 | tf_op jit(solution)/shard_map/all_to_all | solution.py:21
  135.7 1.8 %shard_map.79 = bf16[8,144,256]{2,1,0:T(8,128)(2,1)S(1)} custom-call(s32[1]{0:T(128)} %bitcast.index_ref, bf16[1024,128]{1,0:T(8,128)(2,1)S(1)} %bitcast.14, bf16[1024,128]{1,0:T(8,128)(2,1)S(1)} %collective-permute-done.6.refs_1_, bf16[1024,128]{1,0:T(8,128)(2,1)S(1)} %collective-permute-done.7.refs_2_, ...), custom_call_target="tpu_custom_call" | custom-call | flops 268435456 | bytes 1572864 | tf_op jit(solution)/shard_map/pallas_call | solution.py:43
  137.5 12.4 %all_to_all.33 = bf16[8,144,256]{2,1,0:T(8,128)(2,1)S(1)} all-to-all(bf16[8,144,256]{2,1,0:T(8,128)(2,1)S(1)} %shard_map.79), channel_id=1, replica_groups=mesh['z'=8,'x'=4,'yl'=2,'yh'=2,'core'=2] {'x','yl'}, dimensions={0} | all-to-all | bytes 1179648 | tf_op jit(solution)/shard_map/all_to_all | solution.py:21
  150.0 0.3 copy.13
  150.3 1.0 copy.14
  151.3 0.7 fusion.5
  (5 shorter events, 0.1 us)
Async XLA Ops:
  0.6 5.7 %collective-permute-start.1 = (bf16[32,512]{1,0:T(8,128)(2,1)}, bf16[32,512]{1,0:T(8,128)(2,1)S(1)}, u32[]{:S(2)}, u32[]{:S(2)}) collective-permute-start(bf16[32,512]{1,0:T(8,128)(2,1)} %refs_0_.1), channel_id=1, source_target_pairs={{0,2},{2,0},{1,3},{3,1},{4,6},{6,4},{5,7},{7,5},{8,10},{10,8},{9,1... | collective-permute-start | bytes 98312 | tf_op jit(solution)/shard_map/ppermute | solution.py:29
  2.8 3.6 %collective-permute-start = (bf16[32,512]{1,0:T(8,128)(2,1)}, bf16[32,512]{1,0:T(8,128)(2,1)S(1)}, u32[]{:S(2)}, u32[]{:S(2)}) collective-permute-start(bf16[32,512]{1,0:T(8,128)(2,1)} %refs_0_.1), channel_id=1, source_target_pairs={{0,1},{1,0},{2,3},{3,2},{4,5},{5,4},{6,7},{7,6},{8,9},{9,8},{10,11... | collective-permute-start | bytes 98312 | tf_op jit(solution)/shard_map/ppermute | solution.py:29
  6.3 1.2 collective-permute-start.2
  7.6 0.8 copy-start.3
  29.3 30.9 %copy-start.4 = (bf16[512,8192]{1,0:T(8,128)(2,1)S(1)}, bf16[512,8192]{1,0:T(8,128)(2,1)}, u32[]{:S(2)}) copy-start(bf16[512,8192]{1,0:T(8,128)(2,1)} %param.5) | copy-start | bytes 25165828
  60.3 10.9 %copy-start = (bf16[512,2048]{1,0:T(8,128)(2,1)S(1)}, bf16[512,2048]{1,0:T(8,128)(2,1)}, u32[]{:S(2)}) copy-start(bf16[512,2048]{1,0:T(8,128)(2,1)} %refs_4_.1) | copy-start | bytes 6291460
  60.3 10.9 %copy-start.1 = (f32[8,2048]{1,0:T(8,128)S(1)}, f32[8,2048]{1,0:T(8,128)}, u32[]{:S(2)}) copy-start(f32[8,2048]{1,0:T(8,128)} %refs_5_.1) | copy-start | bytes 196612
  60.3 10.8 %copy-start.2 = (f32[8,2048]{1,0:T(8,128)S(1)}, f32[8,2048]{1,0:T(8,128)}, u32[]{:S(2)}) copy-start(f32[8,2048]{1,0:T(8,128)} %refs_6_.1) | copy-start | bytes 196612
  63.2 6.6 %collective-permute-start.4 = (bf16[128,512]{1,0:T(8,128)(2,1)S(1)}, bf16[128,512]{1,0:T(8,128)(2,1)S(1)}, u32[]{:S(2)}, u32[]{:S(2)}) collective-permute-start(bf16[128,512]{1,0:T(8,128)(2,1)S(1)} %convolution_convert_fusion.refs_0_), channel_id=1, source_target_pairs={{0,2},{2,0},{1,3},{3,1},{4,6},{6,4},{5,7},{7,5},{8,10},{10,8},{9,1... | collective-permute-start | bytes 393224 | tf_op jit(solution)/shard_map/ppermute | solution.py:29
  64.0 5.8 %collective-permute-start.3 = (bf16[128,512]{1,0:T(8,128)(2,1)S(1)}, bf16[128,512]{1,0:T(8,128)(2,1)S(1)}, u32[]{:S(2)}, u32[]{:S(2)}) collective-permute-start(bf16[128,512]{1,0:T(8,128)(2,1)S(1)} %convolution_convert_fusion.refs_0_), channel_id=1, source_target_pairs={{0,1},{1,0},{2,3},{3,2},{4,5},{5,4},{6,7},{7,6},{8,9},{9,8},{10,11... | collective-permute-start | bytes 393224 | tf_op jit(solution)/shard_map/ppermute | solution.py:29
  69.8 1.3 collective-permute-start.5
  107.1 14.0 %all-to-all-start.3 = ((bf16[8,64,256]{2,1,0:T(8,128)(2,1)}), bf16[8,64,256]{2,1,0:T(8,128)(2,1)S(1)}, u32[]{:S(2)}, u32[]{:S(2)}) async-start(bf16[8,64,256]{2,1,0:T(8,128)(2,1)} %bitcast.4), calls=%async_computation.3 | async-start | bytes 524288 | tf_op jit(solution)/shard_map/all_to_all | solution.py:21
  110.5 14.9 %collective-permute-start.7 = (bf16[1024,128]{1,0:T(8,128)(2,1)S(1)}, bf16[1024,128]{1,0:T(8,128)(2,1)S(1)}, u32[]{:S(2)}, u32[]{:S(2)}) collective-permute-start(bf16[1024,128]{1,0:T(8,128)(2,1)S(1)} %bitcast.12), channel_id=1, source_target_pairs={{0,2},{2,0},{1,3},{3,1},{4,6},{6,4},{5,7},{7,5},{8,10},{10,8},{9,1... | collective-permute-start | bytes 786440 | tf_op jit(solution)/shard_map/ppermute | solution.py:29
  121.9 13.8 %all-to-all-start.4 = ((bf16[8,64,256]{2,1,0:T(8,128)(2,1)}), bf16[8,64,256]{2,1,0:T(8,128)(2,1)S(1)}, u32[]{:S(2)}, u32[]{:S(2)}) async-start(bf16[8,64,256]{2,1,0:T(8,128)(2,1)} %broadcast_in_dim.5), calls=%async_computation.4 | async-start | bytes 524288 | tf_op jit(solution)/shard_map/all_to_all | solution.py:21
  125.3 1.6 %collective-permute-start.6 = (bf16[1024,128]{1,0:T(8,128)(2,1)S(1)}, bf16[1024,128]{1,0:T(8,128)(2,1)S(1)}, u32[]{:S(2)}, u32[]{:S(2)}) collective-permute-start(bf16[1024,128]{1,0:T(8,128)(2,1)S(1)} %bitcast.13), channel_id=1, source_target_pairs={{0,1},{1,0},{2,3},{3,2},{4,5},{5,4},{6,7},{7,6},{8,9},{9,8},{10,11... | collective-permute-start | bytes 786440 | tf_op jit(solution)/shard_map/ppermute | solution.py:29
  125.4 1.9 %collective-permute-start.8 = (bf16[1024,128]{1,0:T(8,128)(2,1)S(1)}, bf16[1024,128]{1,0:T(8,128)(2,1)S(1)}, u32[]{:S(2)}, u32[]{:S(2)}) collective-permute-start(bf16[1024,128]{1,0:T(8,128)(2,1)S(1)} %collective-permute-done.7.refs_2_), channel_id=1, source_target_pairs={{0,1},{1,0},{2,3},{3,2},{4,5},{5,4},{6,7},{7,6},{8,9},{9,8},{10,11... | collective-permute-start | bytes 786440 | tf_op jit(solution)/shard_map/ppermute | solution.py:29

commit v3 on v2

--- a/solution.py
+++ b/solution.py
@@ -55,34 +55,77 @@
     )(index, *args)
 
 
-def quarter_copies(index, pieces):
-    rows, rank = pieces[0].shape
-    quarter = rank // NT
-    group = NT * rows
-
-    def kernel(index_ref, *refs):
-        out = refs[-1]
-        for k in range(NT):
-            start = pl.multiple_of((index_ref[0] ^ k) * rows, rows)
-            for z in range(NZ):
-                out[z, pl.ds(start, rows), :] = refs[k][...]
-
-    return call(
-        kernel,
-        index,
-        (1,),
-        [pl.BlockSpec((rows, quarter), lambda i, t: (0, t[0]))] * NT,
-        pl.BlockSpec((NZ, group, quarter), lambda i, t: (0, 0, 0)),
-        jax.ShapeDtypeStruct((NZ, group, quarter), BF16),
-        [],
-        (0, 2 * NZ * group * quarter),
-        16,
-        *pieces,
-    )
-
-
-def coordinates(tokens, plane):
-    part = plane.transpose(1, 0, 2, 3).reshape(tokens.shape[1], plane.shape[3])
+def along(block, shift):
+    return lax.ppermute(block, "x", [(i, (i + shift) % NX) for i in range(NX)])
+
+
+def plane_blocks(line):
+    half = line.shape[0] // 2
+    low, high = line[:half], line[half:]
+    beside = swap(line, "yl")
+    left_low, right_high = along(low, 1), along(high, -1)
+    left_high, right_low = along(high, 1), along(low, -1)
+    far_low, far_high = along(left_low, 1), along(right_high, -1)
+    beside_left, beside_right = along(beside, 1), along(beside, -1)
+    pieces = (
+        (line, 0, 0, 0),
+        (beside, 0, 1, 0),
+        (left_low, NX - 1, 0, 0),
+        (left_high, NX - 1, 0, half),
+        (right_low, 1, 0, 0),
+        (right_high, 1, 0, half),
+        (far_low, 2, 0, 0),
+        (far_high, 2, 0, half),
+        (beside_left, NX - 1, 1, 0),
+        (beside_right, 1, 1, 0),
+        (swap(far_low, "yl"), 2, 1, 0),
+        (swap(far_high, "yl"), 2, 1, half),
+    )
+    place = jnp.stack([lax.axis_index("x"), lax.axis_index("yl")]).astype(jnp.int32)
+
+    def kernel(place_ref, *refs):
+        out, arrived = refs[-2:]
+        copies = []
+        for k, (ref, (_, dx, dy, start)) in enumerate(zip(refs, pieces)):
+            member = ((place_ref[0] + dx) & (NX - 1)) * NYL + (place_ref[1] ^ dy)
+            to = out.at[pl.ds(start, ref.shape[0]), member]
+            copies.append(pltpu.make_async_copy(ref, to, arrived.at[k]))
+        for copy in copies:
+            copy.start()
+        for copy in copies:
+            copy.wait()
+
+    blocks = pl.pallas_call(
+        kernel,
+        in_specs=[pl.BlockSpec(memory_space=pltpu.SMEM)]
+        + [pl.BlockSpec(memory_space=pl.ANY)] * len(pieces),
+        out_specs=pl.BlockSpec(memory_space=pltpu.VMEM),
+        out_shape=jax.ShapeDtypeStruct((line.shape[0], NP) + line.shape[1:], BF16),
+        scratch_shapes=[pltpu.SemaphoreType.DMA((len(pieces),))],
+        compiler_params=pltpu.CompilerParams(vmem_limit_bytes=24 * MIB),
+        cost_estimate=pl.CostEstimate(flops=0, bytes_accessed=4 * NP * line.size, transcendentals=0),
+    )(place, *(piece[0] for piece in pieces))
+    return blocks, beside
+
+
+def loaded(array):
+    def kernel(source, out, arrived):
+        copy = pltpu.make_async_copy(source, out, arrived)
+        copy.start()
+        copy.wait()
+
+    return pl.pallas_call(
+        kernel,
+        in_specs=[pl.BlockSpec(memory_space=pltpu.HBM)],
+        out_specs=pl.BlockSpec(memory_space=pltpu.VMEM),
+        out_shape=jax.ShapeDtypeStruct(array.shape, array.dtype),
+        scratch_shapes=[pltpu.SemaphoreType.DMA],
+        compiler_params=pltpu.CompilerParams(vmem_limit_bytes=24 * MIB),
+        cost_estimate=pl.CostEstimate(flops=0, bytes_accessed=4 * array.size, transcendentals=0),
+    )(array)
+
+def coordinates(tokens, blocks):
+    part = blocks.reshape(tokens.shape[1], blocks.shape[3])
     return jnp.dot(tokens, part, preferred_element_type=F32).astype(BF16).T
 
 
@@ -217,15 +260,19 @@
     part = columns // NP
     index = (NC * lax.axis_index("yh") + lax.axis_index("core")).astype(jnp.int32).reshape(1)
 
-    line = exchange(quarter_copies(index, peers(basis)), ("z",))
-    plane = gather(line, PLANE, NP)
-    coords = peers(coordinates(tokens, plane))
+    pieces = basis.reshape(rows, NT, quarter).transpose(1, 0, 2)
+    pieces = jnp.broadcast_to(pieces[None], (NZ, NT, rows, quarter))
+    line = exchange(pieces.reshape(NZ * NT, rows, quarter), ("z",) + TENSOR)
+    blocks, beside = plane_blocks(line.reshape(NZ, group, quarter))
+    tokens, beside = lax.optimization_barrier((tokens, beside))
+    tokens = loaded(tokens)
+    coords = peers(coordinates(tokens, blocks))
 
     partial = partial_sums(index, coords, grad_out, first_moment, second_moment)
     partial, first_part, second_part = plane_sums(index, exchange(partial, PLANE), own)
 
-    plane, partial = lax.optimization_barrier((plane, partial))
-    rows_here = lax.dynamic_index_in_dim(plane, lax.axis_index("z"), axis=1, keepdims=False)
+    blocks, partial = lax.optimization_barrier((blocks, partial))
+    rows_here = lax.dynamic_index_in_dim(blocks, lax.axis_index("z"), axis=0, keepdims=False)
     rows_here = peers(rows_here.reshape(NP * group, quarter))
 
     partial = exchange(partial.reshape(NZ, NP * own, part), ("z",))

time: 152 us -> 150 us (0.987)
  blocking collectives: 94.9 us -> 67.2 us
  starting transfers between devices: 11 us -> 26.7 us
  local copies, waits for them, and re-layouts: 3.58 us -> 14.4 us
  waiting for transfers between devices: 31.5 us -> 27.9 us
  Pallas kernels: 6.4 us -> 8.02 us
    all_to_all x4 -> x3, blocking collectives: 94.9 us -> 67.2 us  [exchange(): return lax.all_to_all(blocks, axes, 0, 0, tiled=True)]
    ppermute x0 -> x8, starting transfers between devices: none -> 12.5 us  [along(): return lax.ppermute(block, 'x', [(i, (i + shift) % NX) for i in range(NX)])]
    unnamed x11 -> x29, local copies, waits for them, and re-layouts: 1.8 us -> 12.5 us
    ppermute x9, waiting for transfers between devices: 13.3 us -> 7.18 us  [swap(): return lax.ppermute(block, axis, ((0, 1), (1, 0)))]
    ppermute x0 -> x8, waiting for transfers between devices: none -> 3.37 us  [along(): return lax.ppermute(block, 'x', [(i, (i + shift) % NX) for i in range(NX)])]
    ppermute x9, starting transfers between devices: 4.18 us -> 7.41 us  [swap(): return lax.ppermute(block, axis, ((0, 1), (1, 0)))]
    pallas_call x0 -> x2, Pallas kernels: none -> 1.67 us  [the longest x1 1.11 us: plane_blocks(): pl.pallas_call(kernel, in_specs=[pl.BlockSpec(memory_space=pltpu.SMEM)] +...]
    pallas_call x4 -> x3, Pallas kernels: 6.4 us -> 6.34 us  [call(): pl.pallas_call(kernel, grid_spec=pltpu.PrefetchScalarGridSpec(num_scalar_...]
  transfers between devices with their start and end apart: 11 -> 19, of which waited for: 8 -> 9; matrix products, arithmetic and copies ran while one was open for 1% -> 1% of each run, Pallas kernels for 0% -> 0%
where the time goes in v3:
time: 150 us; the launch traced here: 149 us
  blocking collectives  67.2 us (45%)
  waiting for transfers between devices  27.9 us (19%)
  starting transfers between devices  26.7 us (18%)
  local copies, waits for them, and re-layouts  14.4 us (10%)
  Pallas kernels  8.02 us (5%)
  matrix products  2.93 us (2%)
    all_to_all x3, blocking collectives, exchange(): return lax.all_to_all(blocks, axes, 0, 0, tiled=True)  67.2 us
    all_to_all x2, waiting for transfers between devices, exchange(): return lax.all_to_all(blocks, axes, 0, 0, tiled=True)  17.3 us
    ppermute x8, starting transfers between devices, along(): return lax.ppermute(block, 'x', [(i, (i + shift) % NX) for i in range(NX)])  12.5 us
    unnamed x29, local copies, waits for them, and re-layouts  12.5 us
    ppermute x9, starting transfers between devices, swap(): return lax.ppermute(block, axis, ((0, 1), (1, 0)))  7.41 us
    ppermute x9, waiting for transfers between devices, swap(): return lax.ppermute(block, axis, ((0, 1), (1, 0)))  7.18 us
    all_to_all x2, starting transfers between devices, exchange(): return lax.all_to_all(blocks, axes, 0, 0, tiled=True)  6.83 us
    pallas_call x3, Pallas kernels, call(): pl.pallas_call(kernel, grid_spec=pltpu.PrefetchScalarGridSpec(num_scalar_...  6.34 us
  transfers between devices with their start and end apart: 19, of which 9 were waited for; matrix products, arithmetic and copies ran while one was open for 1% of the time, Pallas kernels for 0%

profile of v3, /device:TPU:16, one launch (start us, length us, event | category | flops | bytes accessed | tf_op | source)
XLA Modules:
  0.0 148.8 jit_solution(6284970553350880238)
XLA Ops:
  0.6 0.8 reshape.43
  1.5 23.5 %all_to_all.25 = bf16[32,32,128]{2,1,0:T(8,128)(2,1)S(1)} all-to-all(bf16[32,32,128]{2,1,0:T(8,128)(2,1)S(1)} %bitcast.27), channel_id=1, replica_groups=mesh['z'=8,'x'=4,'yl'=2,'yh'=2,'core'=2] {'z','yh','core'}, dimensions={0} | all-to-all | bytes 524288 | tf_op jit(solution)/shard_map/all_to_all | solution.py:21
  24.9 1.3 collective-permute-start
  26.2 2.8 %collective-permute-start.4 = (bf16[4,128,128]{2,1,0:T(8,128)(2,1)S(1)}, bf16[4,128,128]{2,1,0:T(8,128)(2,1)S(1)}, u32[]{:S(2)}, u32[]{:S(2)}) collective-permute-start(bf16[4,128,128]{2,1,0:T(8,128)(2,1)S(1)} %bitcast.32), channel_id=1, source_target_pairs={{0,24},{8,0},{16,8},{24,16},{1,25},{9,1},{17,9},{25,17},{2,26},{10... | collective-permute-start | bytes 393224 | tf_op jit(solution)/shard_map/ppermute | solution.py:59
  29.1 0.0 collective-permute-start.1
  29.1 0.8 collective-permute-start.2
  29.8 1.8 %collective-permute-done.4.refs_5_ = bf16[4,128,128]{2,1,0:T(8,128)(2,1)S(1)} collective-permute-done((bf16[4,128,128]{2,1,0:T(8,128)(2,1)S(1)}, bf16[4,128,128]{2,1,0:T(8,128)(2,1)S(1)}, u32[]{:S(2)}, u32[]{:S(2)}) %collective-permute-start.4) | collective-permute-done | bytes 131104 | tf_op jit(solution)/shard_map/ppermute | solution.py:59
  31.6 3.7 %collective-permute-start.6 = (bf16[4,128,128]{2,1,0:T(8,128)(2,1)S(1)}, bf16[4,128,128]{2,1,0:T(8,128)(2,1)S(1)}, u32[]{:S(2)}, u32[]{:S(2)}) collective-permute-start(bf16[4,128,128]{2,1,0:T(8,128)(2,1)S(1)} %collective-permute-done.4.refs_5_), channel_id=1, source_target_pairs={{0,24},{8,0},{16,8},{24,16},{1,25},{9,1},{17,9},{25,17},{2,26},{10... | collective-permute-start | bytes 393224 | tf_op jit(solution)/shard_map/ppermute | solution.py:59
  35.3 0.6 collective-permute-done.1.refs_2_
  35.8 0.0 collective-permute-start.5
  35.9 0.0 collective-permute-done.refs_1_
  35.9 0.0 collective-permute-start.7
  35.9 3.3 %collective-permute-start.8 = (bf16[8,128,128]{2,1,0:T(8,128)(2,1)S(1)}, bf16[8,128,128]{2,1,0:T(8,128)(2,1)S(1)}, u32[]{:S(2)}, u32[]{:S(2)}) collective-permute-start(bf16[8,128,128]{2,1,0:T(8,128)(2,1)S(1)} %collective-permute-done.refs_1_), channel_id=1, source_target_pairs={{0,24},{8,0},{16,8},{24,16},{1,25},{9,1},{17,9},{25,17},{2,26},{10... | collective-permute-start | bytes 786440 | tf_op jit(solution)/shard_map/ppermute | solution.py:59
  39.1 0.0 collective-permute-done.2.refs_3_
  39.1 2.0 %collective-permute-start.3 = (bf16[4,128,128]{2,1,0:T(8,128)(2,1)S(1)}, bf16[4,128,128]{2,1,0:T(8,128)(2,1)S(1)}, u32[]{:S(2)}, u32[]{:S(2)}) collective-permute-start(bf16[4,128,128]{2,1,0:T(8,128)(2,1)S(1)} %bitcast.31), channel_id=1, source_target_pairs={{0,24},{8,0},{16,8},{24,16},{1,25},{9,1},{17,9},{25,17},{2,26},{10... | collective-permute-start | bytes 393224 | tf_op jit(solution)/shard_map/ppermute | solution.py:59
  41.1 0.0 collective-permute-done.6.refs_7_
  41.1 0.7 collective-permute-start.10
  41.9 1.0 collective-permute-done.5.refs_6_
  42.9 0.7 collective-permute-start.9
  43.6 0.1 pad_add_fusion.place_ref
  43.7 3.4 %copy-done = bf16[512,8192]{1,0:T(8,128)(2,1)S(1)} copy-done((bf16[512,8192]{1,0:T(8,128)(2,1)S(1)}, bf16[512,8192]{1,0:T(8,128)(2,1)}, u32[]{:S(2)}) %copy-start) | copy-done | bytes 8388632
  47.1 0.6 shard_map.77
  47.7 0.0 collective-permute-done.3.refs_4_
  47.7 0.0 copy-start.8
  47.7 0.6 copy-done.8
  48.3 0.0 collective-permute-done.10.refs_11_
  48.3 0.7 copy-done.10
  49.0 0.0 collective-permute-done.9.refs_10_
  49.0 0.6 copy-done.12
  49.6 0.0 collective-permute-done.7.refs_8_
  49.7 0.9 copy-done.5
  50.6 0.9 copy-done.7
  51.5 0.9 copy-done.9
  52.4 0.9 copy-done.11
  53.3 0.9 copy-done.13
  54.2 1.1 shard_map.76
  55.3 0.0 copy-start.2
  55.3 0.0 copy-start.3
  55.3 2.9 %convolution_convert_fusion.refs_0_ = bf16[128,512]{1,0:T(8,128)(2,1)S(1)} fusion(bf16[8192,128]{1,0:T(8,128)(2,1)S(1)} %bitcast.17, bf16[512,8192]{1,0:T(8,128)(2,1)S(1)} %shard_map.77), kind=kOutput, calls=%fused_computation | convolution fusion | flops 1073807360 | bytes 10616832 | tf_op jit(solution)/shard_map/dot_general | solution.py:129
  58.3 2.1 %collective-permute-start.12 = (bf16[128,512]{1,0:T(8,128)(2,1)S(1)}, bf16[128,512]{1,0:T(8,128)(2,1)S(1)}, u32[]{:S(2)}, u32[]{:S(2)}) collective-permute-start(bf16[128,512]{1,0:T(8,128)(2,1)S(1)} %convolution_convert_fusion.refs_0_), channel_id=1, source_target_pairs={{0,2},{2,0},{1,3},{3,1},{4,6},{6,4},{5,7},{7,5},{8,10},{10,8},{9,1... | collective-permute-start | bytes 393224 | tf_op jit(solution)/shard_map/ppermute | solution.py:29
  60.4 0.0 collective-permute-start.11
  60.4 4.4 %collective-permute-done.12.refs_2_ = bf16[128,512]{1,0:T(8,128)(2,1)S(1)} collective-permute-done((bf16[128,512]{1,0:T(8,128)(2,1)S(1)}, bf16[128,512]{1,0:T(8,128)(2,1)S(1)}, u32[]{:S(2)}, u32[]{:S(2)}) %collective-permute-start.12) | collective-permute-done | bytes 131104 | tf_op jit(solution)/shard_map/ppermute | solution.py:29
  64.8 0.0 collective-permute-start.13
  64.8 1.3 collective-permute-done.13.refs_3_
  66.2 1.6 %copy-done.1 = bf16[512,2048]{1,0:T(8,128)(2,1)S(1)} copy-done((bf16[512,2048]{1,0:T(8,128)(2,1)S(1)}, bf16[512,2048]{1,0:T(8,128)(2,1)}, u32[]{:S(2)}) %copy-start.1) | copy-done | bytes 2097176
  67.8 2.9 %shard_map.78 = bf16[8,544,256]{2,1,0:T(8,128)(2,1)S(1)} custom-call(s32[1]{0:T(128)} %bitcast.index_ref, bf16[128,512]{1,0:T(8,128)(2,1)S(1)} %convolution_convert_fusion.refs_0_, bf16[128,512]{1,0:T(8,128)(2,1)S(1)} %collective-permute-done.11.refs_1_, bf16[128,512]{1,0:T(8,128)(2,1)S(1)} %collective-permute-done.12.refs_2_, ...), custom_call_target="tpu_custom_call" | custom-call | flops 1073741824 | bytes 4325376 | tf_op jit(solution)/shard_map/pallas_call | solution.py:43
  70.6 31.6 %all_to_all.26.sums_ref.moments_ref = bf16[8,544,256]{2,1,0:T(8,128)(2,1)S(1)} all-to-all(bf16[8,544,256]{2,1,0:T(8,128)(2,1)S(1)} %shard_map.78), channel_id=1, replica_groups=mesh['z'=8,'x'=4,'yl'=2,'yh'=2,'core'=2] {'x','yl'}, dimensions={0} | all-to-all | bytes 4456448 | tf_op jit(solution)/shard_map/all_to_all | solution.py:21
  102.2 1.7 %shard_map.79 = (bf16[512,256]{1,0:T(8,128)(2,1)}, f32[64,256]{1,0:T(8,128)S(1)}, f32[64,256]{1,0:T(8,128)S(1)}) custom-call(s32[1]{0:T(128)} %bitcast.index_ref, bf16[8,544,256]{2,1,0:T(8,128)(2,1)S(1)} %all_to_all.26.sums_ref.moments_ref, bf16[8,544,256]{2,1,0:T(8,128)(2,1)S(1)} %all_to_all.26.sums_ref.moments_ref), custom_call_target="tpu_custom_call" | custom-call | flops 1048576 | bytes 2228224 | tf_op jit(solution)/shard_map/pallas_call | solution.py:43
  103.9 3.4 %all-to-all-start.2 = ((bf16[8,64,256]{2,1,0:T(8,128)(2,1)}), bf16[8,64,256]{2,1,0:T(8,128)(2,1)S(1)}, u32[]{:S(2)}, u32[]{:S(2)}) async-start(bf16[8,64,256]{2,1,0:T(8,128)(2,1)} %bitcast.10), calls=%async_computation.2 | async-start | bytes 524288 | tf_op jit(solution)/shard_map/all_to_all | solution.py:21
  107.4 1.9 %collective-permute-start.15 = (bf16[1024,128]{1,0:T(8,128)(2,1)S(1)}, bf16[1024,128]{1,0:T(8,128)(2,1)S(1)}, u32[]{:S(2)}, u32[]{:S(2)}) collective-permute-start(bf16[1024,128]{1,0:T(8,128)(2,1)S(1)} %bitcast.20), channel_id=1, source_target_pairs={{0,2},{2,0},{1,3},{3,1},{4,6},{6,4},{5,7},{7,5},{8,10},{10,8},{9,1... | collective-permute-start | bytes 786440 | tf_op jit(solution)/shard_map/ppermute | solution.py:29
  109.3 8.9 %all-to-all-done.2 = bf16[8,64,256]{2,1,0:T(8,128)(2,1)S(1)} async-done(((bf16[8,64,256]{2,1,0:T(8,128)(2,1)}), bf16[8,64,256]{2,1,0:T(8,128)(2,1)S(1)}, u32[]{:S(2)}, u32[]{:S(2)}) %all-to-all-start.2) | async-done | bytes 262176 | tf_op jit(solution)/shard_map/all_to_all | solution.py:21
  118.3 0.1 fusion.6
  118.3 0.7 broadcast_in_dim.5
  119.0 3.4 %all-to-all-start.3 = ((bf16[8,64,256]{2,1,0:T(8,128)(2,1)}), bf16[8,64,256]{2,1,0:T(8,128)(2,1)S(1)}, u32[]{:S(2)}, u32[]{:S(2)}) async-start(bf16[8,64,256]{2,1,0:T(8,128)(2,1)} %broadcast_in_dim.5), calls=%async_computation.3 | async-start | bytes 524288 | tf_op jit(solution)/shard_map/all_to_all | solution.py:21
  122.5 0.1 collective-permute-start.14
  122.6 0.5 collective-permute-start.16
  123.1 1.0 collective-permute-done.14.refs_1_
  124.1 0.4 collective-permute-done.16.refs_3_
  124.5 8.4 %all-to-all-done.3 = bf16[8,64,256]{2,1,0:T(8,128)(2,1)S(1)} async-done(((bf16[8,64,256]{2,1,0:T(8,128)(2,1)}), bf16[8,64,256]{2,1,0:T(8,128)(2,1)S(1)}, u32[]{:S(2)}, u32[]{:S(2)}) %all-to-all-start.3) | async-done | bytes 262176 | tf_op jit(solution)/shard_map/all_to_all | solution.py:21
  132.8 1.8 %shard_map.80 = bf16[8,144,256]{2,1,0:T(8,128)(2,1)S(1)} custom-call(s32[1]{0:T(128)} %bitcast.index_ref, bf16[1024,128]{1,0:T(8,128)(2,1)S(1)} %bitcast.22, bf16[1024,128]{1,0:T(8,128)(2,1)S(1)} %collective-permute-done.14.refs_1_, bf16[1024,128]{1,0:T(8,128)(2,1)S(1)} %collective-permute-done.15.refs_2_, ...), custom_call_target="tpu_custom_call" | custom-call | flops 268435456 | bytes 1572864 | tf_op jit(solution)/shard_map/pallas_call | solution.py:43
  134.6 12.1 %all_to_all.27 = bf16[8,144,256]{2,1,0:T(8,128)(2,1)S(1)} all-to-all(bf16[8,144,256]{2,1,0:T(8,128)(2,1)S(1)} %shard_map.80), channel_id=1, replica_groups=mesh['z'=8,'x'=4,'yl'=2,'yh'=2,'core'=2] {'x','yl'}, dimensions={0} | all-to-all | bytes 1179648 | tf_op jit(solution)/shard_map/all_to_all | solution.py:21
  146.8 0.3 copy.10
  147.1 1.0 copy.11
  148.1 0.7 fusion.5
  (25 shorter events, 0.2 us)
Async XLA Ops:
  24.9 10.9 %collective-permute-start = (bf16[8,128,128]{2,1,0:T(8,128)(2,1)S(1)}, bf16[8,128,128]{2,1,0:T(8,128)(2,1)S(1)}, u32[]{:S(2)}, u32[]{:S(2)}) collective-permute-start(bf16[8,128,128]{2,1,0:T(8,128)(2,1)S(1)} %bitcast.18), channel_id=1, source_target_pairs={{0,4},{4,0},{1,5},{5,1},{2,6},{6,2},{3,7},{7,3},{8,12},{12,8},{9,1... | collective-permute-start | bytes 786440 | tf_op jit(solution)/shard_map/ppermute | solution.py:29
  26.2 5.4 %collective-permute-start.4 = (bf16[4,128,128]{2,1,0:T(8,128)(2,1)S(1)}, bf16[4,128,128]{2,1,0:T(8,128)(2,1)S(1)}, u32[]{:S(2)}, u32[]{:S(2)}) collective-permute-start(bf16[4,128,128]{2,1,0:T(8,128)(2,1)S(1)} %bitcast.32), channel_id=1, source_target_pairs={{0,24},{8,0},{16,8},{24,16},{1,25},{9,1},{17,9},{25,17},{2,26},{10... | collective-permute-start | bytes 393224 | tf_op jit(solution)/shard_map/ppermute | solution.py:59
  29.1 6.8 %collective-permute-start.1 = (bf16[4,128,128]{2,1,0:T(8,128)(2,1)S(1)}, bf16[4,128,128]{2,1,0:T(8,128)(2,1)S(1)}, u32[]{:S(2)}, u32[]{:S(2)}) collective-permute-start(bf16[4,128,128]{2,1,0:T(8,128)(2,1)S(1)} %bitcast.30), channel_id=1, source_target_pairs={{0,8},{8,16},{16,24},{24,0},{1,9},{9,17},{17,25},{25,1},{2,10},{10... | collective-permute-start | bytes 393224 | tf_op jit(solution)/shard_map/ppermute | solution.py:59
  29.1 10.0 %collective-permute-start.2 = (bf16[4,128,128]{2,1,0:T(8,128)(2,1)S(1)}, bf16[4,128,128]{2,1,0:T(8,128)(2,1)S(1)}, u32[]{:S(2)}, u32[]{:S(2)}) collective-permute-start(bf16[4,128,128]{2,1,0:T(8,128)(2,1)S(1)} %bitcast.33), channel_id=1, source_target_pairs={{0,8},{8,16},{16,24},{24,0},{1,9},{9,17},{17,25},{25,1},{2,10},{10... | collective-permute-start | bytes 393224 | tf_op jit(solution)/shard_map/ppermute | solution.py:59
  31.6 9.5 %collective-permute-start.6 = (bf16[4,128,128]{2,1,0:T(8,128)(2,1)S(1)}, bf16[4,128,128]{2,1,0:T(8,128)(2,1)S(1)}, u32[]{:S(2)}, u32[]{:S(2)}) collective-permute-start(bf16[4,128,128]{2,1,0:T(8,128)(2,1)S(1)} %collective-permute-done.4.refs_5_), channel_id=1, source_target_pairs={{0,24},{8,0},{16,8},{24,16},{1,25},{9,1},{17,9},{25,17},{2,26},{10... | collective-permute-start | bytes 393224 | tf_op jit(solution)/shard_map/ppermute | solution.py:59
  35.8 7.0 %collective-permute-start.5 = (bf16[4,128,128]{2,1,0:T(8,128)(2,1)S(1)}, bf16[4,128,128]{2,1,0:T(8,128)(2,1)S(1)}, u32[]{:S(2)}, u32[]{:S(2)}) collective-permute-start(bf16[4,128,128]{2,1,0:T(8,128)(2,1)S(1)} %collective-permute-done.1.refs_2_), channel_id=1, source_target_pairs={{0,8},{8,16},{16,24},{24,0},{1,9},{9,17},{17,25},{25,1},{2,10},{10... | collective-permute-start | bytes 393224 | tf_op jit(solution)/shard_map/ppermute | solution.py:59
  35.9 13.8 %collective-permute-start.7 = (bf16[8,128,128]{2,1,0:T(8,128)(2,1)S(1)}, bf16[8,128,128]{2,1,0:T(8,128)(2,1)S(1)}, u32[]{:S(2)}, u32[]{:S(2)}) collective-permute-start(bf16[8,128,128]{2,1,0:T(8,128)(2,1)S(1)} %collective-permute-done.refs_1_), channel_id=1, source_target_pairs={{0,8},{8,16},{16,24},{24,0},{1,9},{9,17},{17,25},{25,1},{2,10},{10... | collective-permute-start | bytes 786440 | tf_op jit(solution)/shard_map/ppermute | solution.py:59
  35.9 13.8 %collective-permute-start.8 = (bf16[8,128,128]{2,1,0:T(8,128)(2,1)S(1)}, bf16[8,128,128]{2,1,0:T(8,128)(2,1)S(1)}, u32[]{:S(2)}, u32[]{:S(2)}) collective-permute-start(bf16[8,128,128]{2,1,0:T(8,128)(2,1)S(1)} %collective-permute-done.refs_1_), channel_id=1, source_target_pairs={{0,24},{8,0},{16,8},{24,16},{1,25},{9,1},{17,9},{25,17},{2,26},{10... | collective-permute-start | bytes 786440 | tf_op jit(solution)/shard_map/ppermute | solution.py:59
  39.1 8.5 %collective-permute-start.3 = (bf16[4,128,128]{2,1,0:T(8,128)(2,1)S(1)}, bf16[4,128,128]{2,1,0:T(8,128)(2,1)S(1)}, u32[]{:S(2)}, u32[]{:S(2)}) collective-permute-start(bf16[4,128,128]{2,1,0:T(8,128)(2,1)S(1)} %bitcast.31), channel_id=1, source_target_pairs={{0,24},{8,0},{16,8},{24,16},{1,25},{9,1},{17,9},{25,17},{2,26},{10... | collective-permute-start | bytes 393224 | tf_op jit(solution)/shard_map/ppermute | solution.py:59
  41.1 6.5 %copy-start.4 = (bf16[4,128,128]{2,1,0:T(8,128)(2,1)}, bf16[4,128,128]{2,1,0:T(8,128)(2,1)S(1)}, u32[]{:S(2)}) copy-start(bf16[4,128,128]{2,1,0:T(8,128)(2,1)S(1)} %collective-permute-done.6.refs_7_) | copy-start | bytes 393220
  41.1 7.2 %collective-permute-start.10 = (bf16[4,128,128]{2,1,0:T(8,128)(2,1)S(1)}, bf16[4,128,128]{2,1,0:T(8,128)(2,1)S(1)}, u32[]{:S(2)}, u32[]{:S(2)}) collective-permute-start(bf16[4,128,128]{2,1,0:T(8,128)(2,1)S(1)} %collective-permute-done.6.refs_7_), channel_id=1, source_target_pairs={{0,4},{4,0},{1,5},{5,1},{2,6},{6,2},{3,7},{7,3},{8,12},{12,8},{9,1... | collective-permute-start | bytes 393224 | tf_op jit(solution)/shard_map/ppermute | solution.py:29
  42.9 4.8 %copy-start.6 = (bf16[4,128,128]{2,1,0:T(8,128)(2,1)}, bf16[4,128,128]{2,1,0:T(8,128)(2,1)S(1)}, u32[]{:S(2)}) copy-start(bf16[4,128,128]{2,1,0:T(8,128)(2,1)S(1)} %collective-permute-done.5.refs_6_) | copy-start | bytes 393220
  42.9 6.1 %collective-permute-start.9 = (bf16[4,128,128]{2,1,0:T(8,128)(2,1)S(1)}, bf16[4,128,128]{2,1,0:T(8,128)(2,1)S(1)}, u32[]{:S(2)}, u32[]{:S(2)}) collective-permute-start(bf16[4,128,128]{2,1,0:T(8,128)(2,1)S(1)} %collective-permute-done.5.refs_6_), channel_id=1, source_target_pairs={{0,4},{4,0},{1,5},{5,1},{2,6},{6,2},{3,7},{7,3},{8,12},{12,8},{9,1... | collective-permute-start | bytes 393224 | tf_op jit(solution)/shard_map/ppermute | solution.py:29
  43.7 3.4 %copy-start = (bf16[512,8192]{1,0:T(8,128)(2,1)S(1)}, bf16[512,8192]{1,0:T(8,128)(2,1)}, u32[]{:S(2)}) copy-start(bf16[512,8192]{1,0:T(8,128)(2,1)} %source) | copy-start | bytes 25165828
  47.7 0.7 copy-start.8
  48.3 0.7 copy-start.10
  49.0 0.6 copy-start.12
  49.7 0.9 copy-start.5
  50.6 0.9 copy-start.7
  51.5 0.9 copy-start.9
  52.4 0.9 copy-start.11
  53.3 0.9 copy-start.13
  55.3 10.9 %copy-start.2 = (f32[8,2048]{1,0:T(8,128)S(1)}, f32[8,2048]{1,0:T(8,128)}, u32[]{:S(2)}) copy-start(f32[8,2048]{1,0:T(8,128)} %refs_5_.1) | copy-start | bytes 196612
  55.3 10.9 %copy-start.3 = (f32[8,2048]{1,0:T(8,128)S(1)}, f32[8,2048]{1,0:T(8,128)}, u32[]{:S(2)}) copy-start(f32[8,2048]{1,0:T(8,128)} %refs_6_.1) | copy-start | bytes 196612
  58.3 6.6 %collective-permute-start.12 = (bf16[128,512]{1,0:T(8,128)(2,1)S(1)}, bf16[128,512]{1,0:T(8,128)(2,1)S(1)}, u32[]{:S(2)}, u32[]{:S(2)}) collective-permute-start(bf16[128,512]{1,0:T(8,128)(2,1)S(1)} %convolution_convert_fusion.refs_0_), channel_id=1, source_target_pairs={{0,2},{2,0},{1,3},{3,1},{4,6},{6,4},{5,7},{7,5},{8,10},{10,8},{9,1... | collective-permute-start | bytes 393224 | tf_op jit(solution)/shard_map/ppermute | solution.py:29
  60.4 4.4 %collective-permute-start.11 = (bf16[128,512]{1,0:T(8,128)(2,1)S(1)}, bf16[128,512]{1,0:T(8,128)(2,1)S(1)}, u32[]{:S(2)}, u32[]{:S(2)}) collective-permute-start(bf16[128,512]{1,0:T(8,128)(2,1)S(1)} %convolution_convert_fusion.refs_0_), channel_id=1, source_target_pairs={{0,1},{1,0},{2,3},{3,2},{4,5},{5,4},{6,7},{7,6},{8,9},{9,8},{10,11... | collective-permute-start | bytes 393224 | tf_op jit(solution)/shard_map/ppermute | solution.py:29
  64.8 1.3 collective-permute-start.13
  66.2 1.6 %copy-start.1 = (bf16[512,2048]{1,0:T(8,128)(2,1)S(1)}, bf16[512,2048]{1,0:T(8,128)(2,1)}, u32[]{:S(2)}) copy-start(bf16[512,2048]{1,0:T(8,128)(2,1)} %refs_4_.1) | copy-start | bytes 6291460
  103.9 14.3 %all-to-all-start.2 = ((bf16[8,64,256]{2,1,0:T(8,128)(2,1)}), bf16[8,64,256]{2,1,0:T(8,128)(2,1)S(1)}, u32[]{:S(2)}, u32[]{:S(2)}) async-start(bf16[8,64,256]{2,1,0:T(8,128)(2,1)} %bitcast.10), calls=%async_computation.2 | async-start | bytes 524288 | tf_op jit(solution)/shard_map/all_to_all | solution.py:21
  107.4 15.2 %collective-permute-start.15 = (bf16[1024,128]{1,0:T(8,128)(2,1)S(1)}, bf16[1024,128]{1,0:T(8,128)(2,1)S(1)}, u32[]{:S(2)}, u32[]{:S(2)}) collective-permute-start(bf16[1024,128]{1,0:T(8,128)(2,1)S(1)} %bitcast.20), channel_id=1, source_target_pairs={{0,2},{2,0},{1,3},{3,1},{4,6},{6,4},{5,7},{7,5},{8,10},{10,8},{9,1... | collective-permute-start | bytes 786440 | tf_op jit(solution)/shard_map/ppermute | solution.py:29
  119.0 13.8 %all-to-all-start.3 = ((bf16[8,64,256]{2,1,0:T(8,128)(2,1)}), bf16[8,64,256]{2,1,0:T(8,128)(2,1)S(1)}, u32[]{:S(2)}, u32[]{:S(2)}) async-start(bf16[8,64,256]{2,1,0:T(8,128)(2,1)} %broadcast_in_dim.5), calls=%async_computation.3 | async-start | bytes 524288 | tf_op jit(solution)/shard_map/all_to_all | solution.py:21
  122.5 1.6 %collective-permute-start.14 = (bf16[1024,128]{1,0:T(8,128)(2,1)S(1)}, bf16[1024,128]{1,0:T(8,128)(2,1)S(1)}, u32[]{:S(2)}, u32[]{:S(2)}) collective-permute-start(bf16[1024,128]{1,0:T(8,128)(2,1)S(1)} %bitcast.21), channel_id=1, source_target_pairs={{0,1},{1,0},{2,3},{3,2},{4,5},{5,4},{6,7},{7,6},{8,9},{9,8},{10,11... | collective-permute-start | bytes 786440 | tf_op jit(solution)/shard_map/ppermute | solution.py:29
  122.6 1.9 %collective-permute-start.16 = (bf16[1024,128]{1,0:T(8,128)(2,1)S(1)}, bf16[1024,128]{1,0:T(8,128)(2,1)S(1)}, u32[]{:S(2)}, u32[]{:S(2)}) collective-permute-start(bf16[1024,128]{1,0:T(8,128)(2,1)S(1)} %collective-permute-done.15.refs_2_), channel_id=1, source_target_pairs={{0,1},{1,0},{2,3},{3,2},{4,5},{5,4},{6,7},{7,6},{8,9},{9,8},{10,11... | collective-permute-start | bytes 786440 | tf_op jit(solution)/shard_map/ppermute | solution.py:29

commit v4 on v3

--- a/solution.py
+++ b/solution.py
@@ -13,6 +13,7 @@
 NZ, NX, NYL, NYH, NC = 8, 4, 2, 2, 2
 NP = NX * NYL
 NT = NYH * NC
+PAIR = 2
 MIB = 1024 * 1024
 F32, BF16 = jnp.float32, jnp.bfloat16
 
@@ -61,19 +62,14 @@
 
 def plane_blocks(line):
     half = line.shape[0] // 2
-    low, high = line[:half], line[half:]
-    beside = swap(line, "yl")
-    left_low, right_high = along(low, 1), along(high, -1)
-    left_high, right_low = along(high, 1), along(low, -1)
-    far_low, far_high = along(left_low, 1), along(right_high, -1)
+    beside, left, right = swap(line, "yl"), along(line, 1), along(line, -1)
+    far_low, far_high = along(left[:half], 1), along(right[half:], -1)
     beside_left, beside_right = along(beside, 1), along(beside, -1)
     pieces = (
         (line, 0, 0, 0),
         (beside, 0, 1, 0),
-        (left_low, NX - 1, 0, 0),
-        (left_high, NX - 1, 0, half),
-        (right_low, 1, 0, 0),
-        (right_high, 1, 0, half),
+        (left, NX - 1, 0, 0),
+        (right, 1, 0, 0),
         (far_low, 2, 0, 0),
         (far_high, 2, 0, half),
         (beside_left, NX - 1, 1, 0),
@@ -81,48 +77,39 @@
         (swap(far_low, "yl"), 2, 1, 0),
         (swap(far_high, "yl"), 2, 1, half),
     )
-    place = jnp.stack([lax.axis_index("x"), lax.axis_index("yl")]).astype(jnp.int32)
-
-    def kernel(place_ref, *refs):
-        out, arrived = refs[-2:]
-        copies = []
-        for k, (ref, (_, dx, dy, start)) in enumerate(zip(refs, pieces)):
-            member = ((place_ref[0] + dx) & (NX - 1)) * NYL + (place_ref[1] ^ dy)
-            to = out.at[pl.ds(start, ref.shape[0]), member]
-            copies.append(pltpu.make_async_copy(ref, to, arrived.at[k]))
+    x, yl = lax.axis_index("x"), lax.axis_index("yl")
+    blocks = jnp.zeros((line.shape[0], NP) + line.shape[1:], BF16)
+    for piece, dx, dy, start in pieces:
+        member = ((x + dx) & (NX - 1)) * NYL + (yl ^ dy)
+        blocks = lax.dynamic_update_slice(blocks, piece[:, None], (start, member, 0, 0))
+    return blocks, beside
+
+
+def loaded(*arrays):
+    count = len(arrays)
+
+    def kernel(*refs):
+        sources, outs, arrived = refs[:count], refs[count:-1], refs[-1]
+        copies = [
+            pltpu.make_async_copy(sources[k], outs[k], arrived.at[k]) for k in range(count)
+        ]
         for copy in copies:
             copy.start()
         for copy in copies:
             copy.wait()
 
-    blocks = pl.pallas_call(
-        kernel,
-        in_specs=[pl.BlockSpec(memory_space=pltpu.SMEM)]
-        + [pl.BlockSpec(memory_space=pl.ANY)] * len(pieces),
-        out_specs=pl.BlockSpec(memory_space=pltpu.VMEM),
-        out_shape=jax.ShapeDtypeStruct((line.shape[0], NP) + line.shape[1:], BF16),
-        scratch_shapes=[pltpu.SemaphoreType.DMA((len(pieces),))],
-        compiler_params=pltpu.CompilerParams(vmem_limit_bytes=24 * MIB),
-        cost_estimate=pl.CostEstimate(flops=0, bytes_accessed=4 * NP * line.size, transcendentals=0),
-    )(place, *(piece[0] for piece in pieces))
-    return blocks, beside
-
-
-def loaded(array):
-    def kernel(source, out, arrived):
-        copy = pltpu.make_async_copy(source, out, arrived)
-        copy.start()
-        copy.wait()
-
     return pl.pallas_call(
         kernel,
-        in_specs=[pl.BlockSpec(memory_space=pltpu.HBM)],
-        out_specs=pl.BlockSpec(memory_space=pltpu.VMEM),
-        out_shape=jax.ShapeDtypeStruct(array.shape, array.dtype),
-        scratch_shapes=[pltpu.SemaphoreType.DMA],
-        compiler_params=pltpu.CompilerParams(vmem_limit_bytes=24 * MIB),
-        cost_estimate=pl.CostEstimate(flops=0, bytes_accessed=4 * array.size, transcendentals=0),
-    )(array)
+        in_specs=[pl.BlockSpec(memory_space=pltpu.HBM)] * count,
+        out_specs=[pl.BlockSpec(memory_space=pltpu.VMEM)] * count,
+        out_shape=[jax.ShapeDtypeStruct(array.shape, array.dtype) for array in arrays],
+        scratch_shapes=[pltpu.SemaphoreType.DMA((count,))],
+        compiler_params=pltpu.CompilerParams(vmem_limit_bytes=40 * MIB),
+        cost_estimate=pl.CostEstimate(
+            flops=0, bytes_accessed=4 * sum(array.size for array in arrays), transcendentals=0
+        ),
+    )(*arrays)
+
 
 def coordinates(tokens, blocks):
     part = blocks.reshape(tokens.shape[1], blocks.shape[3])
@@ -137,22 +124,24 @@
 
     def kernel(index_ref, *refs):
         pieces, (grad_ref, first_ref, second_ref, out) = refs[:NT], refs[NT:]
-        for k in range(NT):
-            start = pl.multiple_of((index_ref[0] ^ k) * quarter, quarter)
-            out[0, pl.ds(start, quarter), :] = jnp.dot(
-                pieces[k][...], grad_ref[...], preferred_element_type=F32
-            ).astype(BF16)
-        out[0, rank : rank + 2 * own, :] = jnp.concatenate(halves(first_ref[...]))
-        out[0, rank + 2 * own :, :] = jnp.concatenate(halves(second_ref[...]))
+        for j in range(PAIR):
+            here = slice(j * part, (j + 1) * part)
+            for k in range(NT):
+                start = pl.multiple_of((index_ref[0] ^ k) * quarter, quarter)
+                out[j, pl.ds(start, quarter), :] = jnp.dot(
+                    pieces[k][...], grad_ref[:, here], preferred_element_type=F32
+                ).astype(BF16)
+            out[j, rank : rank + 2 * own, :] = jnp.concatenate(halves(first_ref[:, here]))
+            out[j, rank + 2 * own :, :] = jnp.concatenate(halves(second_ref[:, here]))
 
     return call(
         kernel,
         index,
-        (NP,),
+        (NP // PAIR,),
         [pl.BlockSpec((quarter, count), lambda p, t: (0, 0))] * NT
-        + [pl.BlockSpec((count, part), lambda p, t: (0, p))]
-        + [pl.BlockSpec((own, part), lambda p, t: (0, p))] * 2,
-        pl.BlockSpec((1, rows, part), lambda p, t: (p, 0, 0)),
+        + [pl.BlockSpec((count, PAIR * part), lambda p, t: (0, p))]
+        + [pl.BlockSpec((own, PAIR * part), lambda p, t: (0, p))] * 2,
+        pl.BlockSpec((PAIR, rows, part), lambda p, t: (p, 0, 0)),
         jax.ShapeDtypeStruct((NP, rows, part), BF16),
         [],
         (2 * rank * count * columns, 2 * columns * (count + rows)),
@@ -265,7 +254,7 @@
     line = exchange(pieces.reshape(NZ * NT, rows, quarter), ("z",) + TENSOR)
     blocks, beside = plane_blocks(line.reshape(NZ, group, quarter))
     tokens, beside = lax.optimization_barrier((tokens, beside))
-    tokens = loaded(tokens)
+    (tokens,) = loaded(tokens)
     coords = peers(coordinates(tokens, blocks))
 
     partial = partial_sums(index, coords, grad_out, first_moment, second_moment)

time: 150 us -> 143 us (0.953)
  local copies, waits for them, and re-layouts: 14.4 us -> 4.68 us
  waiting for transfers between devices: 27.9 us -> 30.8 us
  starting transfers between devices: 26.7 us -> 25 us
    unnamed x29 -> x9, local copies, waits for them, and re-layouts: 12.5 us -> 1.04 us
    ppermute x8 -> x6, starting transfers between devices: 12.5 us -> 9.93 us  [along(): return lax.ppermute(block, 'x', [(i, (i + shift) % NX) for i in range(NX)])]
    ppermute x8 -> x6, waiting for transfers between devices: 3.37 us -> 5.7 us  [along(): return lax.ppermute(block, 'x', [(i, (i + shift) % NX) for i in range(NX)])]
    ppermute x9, waiting for transfers between devices: 7.18 us -> 9.31 us  [swap(): return lax.ppermute(block, axis, ((0, 1), (1, 0)))]
    pallas_call x2 -> x1, Pallas kernels: 1.67 us -> 3.39 us  [loaded(): pl.pallas_call(kernel, in_specs=[pl.BlockSpec(memory_space=pltpu.HBM)] *...]
    all_to_all x2, waiting for transfers between devices: 17.3 us -> 15.8 us  [exchange(): return lax.all_to_all(blocks, axes, 0, 0, tiled=True)]
  transfers between devices with their start and end apart: 19 -> 17, of which waited for: 9 -> 10; matrix products, arithmetic and copies ran while one was open for 1% -> 2% of each run, Pallas kernels for 0% -> 2%
where the time goes in v4:
time: 143 us; the launch traced here: 141 us
  blocking collectives  67.2 us (47%)
  waiting for transfers between devices  30.8 us (22%)
  starting transfers between devices  25 us (17%)
  Pallas kernels  8.89 us (6%)
  local copies, waits for them, and re-layouts  4.68 us (3%)
  matrix products  2.9 us (2%)
    all_to_all x3, blocking collectives, exchange(): return lax.all_to_all(blocks, axes, 0, 0, tiled=True)  67.2 us
    all_to_all x2, waiting for transfers between devices, exchange(): return lax.all_to_all(blocks, axes, 0, 0, tiled=True)  15.8 us
    ppermute x6, starting transfers between devices, along(): return lax.ppermute(block, 'x', [(i, (i + shift) % NX) for i in range(NX)])  9.93 us
    ppermute x9, waiting for transfers between devices, swap(): return lax.ppermute(block, axis, ((0, 1), (1, 0)))  9.31 us
    ppermute x9, starting transfers between devices, swap(): return lax.ppermute(block, axis, ((0, 1), (1, 0)))  8.27 us
    all_to_all x2, starting transfers between devices, exchange(): return lax.all_to_all(blocks, axes, 0, 0, tiled=True)  6.83 us
    ppermute x6, waiting for transfers between devices, along(): return lax.ppermute(block, 'x', [(i, (i + shift) % NX) for i in range(NX)])  5.7 us
    pallas_call x3, Pallas kernels, call(): pl.pallas_call(kernel, grid_spec=pltpu.PrefetchScalarGridSpec(num_scalar_...  5.5 us
  transfers between devices with their start and end apart: 17, of which 10 were waited for; matrix products, arithmetic and copies ran while one was open for 2% of the time, Pallas kernels for 2%

profile of v4, /device:TPU:16, one launch (start us, length us, event | category | flops | bytes accessed | tf_op | source)
XLA Modules:
  0.0 141.2 jit_solution(1568580019542724073)
XLA Ops:
  0.6 0.8 reshape.41
  1.5 23.5 %all_to_all.25 = bf16[32,32,128]{2,1,0:T(8,128)(2,1)S(1)} all-to-all(bf16[32,32,128]{2,1,0:T(8,128)(2,1)S(1)} %bitcast.60), channel_id=1, replica_groups=mesh['z'=8,'x'=4,'yl'=2,'yh'=2,'core'=2] {'z','yh','core'}, dimensions={0} | all-to-all | bytes 524288 | tf_op jit(solution)/shard_map/all_to_all | solution.py:22
  24.9 1.5 %collective-permute-start.1 = (bf16[8,128,128]{2,1,0:T(8,128)(2,1)S(1)}, bf16[8,128,128]{2,1,0:T(8,128)(2,1)S(1)}, u32[]{:S(2)}, u32[]{:S(2)}) collective-permute-start(bf16[8,128,128]{2,1,0:T(8,128)(2,1)S(1)} %bitcast.56), channel_id=1, source_target_pairs={{0,8},{8,16},{16,24},{24,0},{1,9},{9,17},{17,25},{25,1},{2,10},{10... | collective-permute-start | bytes 786440 | tf_op jit(solution)/shard_map/ppermute | solution.py:60
  26.4 1.7 %collective-permute-start.2 = (bf16[8,128,128]{2,1,0:T(8,128)(2,1)S(1)}, bf16[8,128,128]{2,1,0:T(8,128)(2,1)S(1)}, u32[]{:S(2)}, u32[]{:S(2)}) collective-permute-start(bf16[8,128,128]{2,1,0:T(8,128)(2,1)S(1)} %bitcast.57), channel_id=1, source_target_pairs={{0,24},{8,0},{16,8},{24,16},{1,25},{9,1},{17,9},{25,17},{2,26},{10... | collective-permute-start | bytes 786440 | tf_op jit(solution)/shard_map/ppermute | solution.py:60
  28.2 1.3 collective-permute-start
  29.5 0.5 broadcast_in_dim.42
  30.0 3.7 %collective-permute-done.1 = bf16[8,128,128]{2,1,0:T(8,128)(2,1)S(1)} collective-permute-done((bf16[8,128,128]{2,1,0:T(8,128)(2,1)S(1)}, bf16[8,128,128]{2,1,0:T(8,128)(2,1)S(1)}, u32[]{:S(2)}, u32[]{:S(2)}) %collective-permute-start.1) | collective-permute-done | bytes 262176 | tf_op jit(solution)/shard_map/ppermute | solution.py:60
  33.7 0.4 collective-permute-start.3
  34.0 0.0 collective-permute-done.2
  34.1 3.0 %collective-permute-start.4 = (bf16[4,128,128]{2,1,0:T(8,128)(2,1)S(1)}, bf16[4,128,128]{2,1,0:T(8,128)(2,1)S(1)}, u32[]{:S(2)}, u32[]{:S(2)}) collective-permute-start(bf16[4,128,128]{2,1,0:T(8,128)(2,1)S(1)} %slice.27), channel_id=1, source_target_pairs={{0,24},{8,0},{16,8},{24,16},{1,25},{9,1},{17,9},{25,17},{2,26},{10... | collective-permute-start | bytes 393224 | tf_op jit(solution)/shard_map/ppermute | solution.py:60
  37.1 0.0 collective-permute-done
  37.1 3.4 %shard_map.76 = bf16[512,8192]{1,0:T(8,128)(2,1)S(1)} custom-call(bf16[512,8192]{1,0:T(8,128)(2,1)} %refs_0_), custom_call_target="tpu_custom_call" | custom-call | bytes 16777216 | tf_op jit(solution)/shard_map/pallas_call | solution.py:101
  40.5 0.1 collective-permute-start.5
  40.6 3.2 %collective-permute-start.6 = (bf16[8,128,128]{2,1,0:T(8,128)(2,1)S(1)}, bf16[8,128,128]{2,1,0:T(8,128)(2,1)S(1)}, u32[]{:S(2)}, u32[]{:S(2)}) collective-permute-start(bf16[8,128,128]{2,1,0:T(8,128)(2,1)S(1)} %collective-permute-done), channel_id=1, source_target_pairs={{0,24},{8,0},{16,8},{24,16},{1,25},{9,1},{17,9},{25,17},{2,26},{10... | collective-permute-start | bytes 786440 | tf_op jit(solution)/shard_map/ppermute | solution.py:60
  43.9 0.0 collective-permute-done.3
  44.0 1.4 collective-permute-start.7
  45.3 0.0 collective-permute-done.4
  45.3 0.7 collective-permute-start.8
  46.1 2.0 %collective-permute-done.5 = bf16[8,128,128]{2,1,0:T(8,128)(2,1)S(1)} collective-permute-done((bf16[8,128,128]{2,1,0:T(8,128)(2,1)S(1)}, bf16[8,128,128]{2,1,0:T(8,128)(2,1)S(1)}, u32[]{:S(2)}, u32[]{:S(2)}) %collective-permute-start.5) | collective-permute-done | bytes 262176 | tf_op jit(solution)/shard_map/ppermute | solution.py:60
  48.2 0.0 collective-permute-done.6
  48.3 0.8 collective-permute-done.7
  49.0 1.4 collective-permute-done.8
  50.4 0.0 copy-start.3
  50.4 0.0 copy-start
  50.5 0.0 copy-start.1
  50.5 0.0 copy-start.2
  50.5 2.9 %convolution_convert_fusion.refs_0_ = bf16[128,512]{1,0:T(8,128)(2,1)S(1)} fusion(bf16[8192,128]{1,0:T(8,128)(2,1)S(1)} %bitcast.52, bf16[512,8192]{1,0:T(8,128)(2,1)S(1)} %shard_map.76), kind=kOutput, calls=%fused_computation | convolution fusion | flops 1073807360 | bytes 10616832 | tf_op jit(solution)/shard_map/dot_general | solution.py:116
  53.4 0.0 copy-done.3
  53.4 2.1 %collective-permute-start.10 = (bf16[128,512]{1,0:T(8,128)(2,1)S(1)}, bf16[128,512]{1,0:T(8,128)(2,1)S(1)}, u32[]{:S(2)}, u32[]{:S(2)}) collective-permute-start(bf16[128,512]{1,0:T(8,128)(2,1)S(1)} %convolution_convert_fusion.refs_0_), channel_id=1, source_target_pairs={{0,2},{2,0},{1,3},{3,1},{4,6},{6,4},{5,7},{7,5},{8,10},{10,8},{9,1... | collective-permute-start | bytes 393224 | tf_op jit(solution)/shard_map/ppermute | solution.py:30
  55.5 0.0 collective-permute-start.9
  55.5 4.4 %collective-permute-done.10.refs_2_ = bf16[128,512]{1,0:T(8,128)(2,1)S(1)} collective-permute-done((bf16[128,512]{1,0:T(8,128)(2,1)S(1)}, bf16[128,512]{1,0:T(8,128)(2,1)S(1)}, u32[]{:S(2)}, u32[]{:S(2)}) %collective-permute-start.10) | collective-permute-done | bytes 131104 | tf_op jit(solution)/shard_map/ppermute | solution.py:30
  60.0 0.0 collective-permute-start.11
  60.0 0.0 collective-permute-done.9.refs_1_
  60.0 1.3 collective-permute-done.11.refs_3_
  61.3 0.0 copy-done
  61.3 0.0 copy-done.1
  61.3 0.0 copy-done.2
  61.3 2.0 %shard_map.77 = bf16[8,544,256]{2,1,0:T(8,128)(2,1)S(1)} custom-call(s32[1]{0:T(128)} %bitcast.index_ref, bf16[128,512]{1,0:T(8,128)(2,1)S(1)} %convolution_convert_fusion.refs_0_, bf16[128,512]{1,0:T(8,128)(2,1)S(1)} %collective-permute-done.9.refs_1_, bf16[128,512]{1,0:T(8,128)(2,1)S(1)} %collective-permute-done.10.refs_2_, ...), custom_call_target="tpu_custom_call" | custom-call | flops 1073741824 | bytes 4325376 | tf_op jit(solution)/shard_map/pallas_call | solution.py:44
  63.4 31.3 %all_to_all.26.sums_ref.moments_ref = bf16[8,544,256]{2,1,0:T(8,128)(2,1)S(1)} all-to-all(bf16[8,544,256]{2,1,0:T(8,128)(2,1)S(1)} %shard_map.77), channel_id=1, replica_groups=mesh['z'=8,'x'=4,'yl'=2,'yh'=2,'core'=2] {'x','yl'}, dimensions={0} | all-to-all | bytes 4456448 | tf_op jit(solution)/shard_map/all_to_all | solution.py:22
  94.7 1.7 %shard_map.78 = (bf16[512,256]{1,0:T(8,128)(2,1)}, f32[64,256]{1,0:T(8,128)S(1)}, f32[64,256]{1,0:T(8,128)S(1)}) custom-call(s32[1]{0:T(128)} %bitcast.index_ref, bf16[8,544,256]{2,1,0:T(8,128)(2,1)S(1)} %all_to_all.26.sums_ref.moments_ref, bf16[8,544,256]{2,1,0:T(8,128)(2,1)S(1)} %all_to_all.26.sums_ref.moments_ref), custom_call_target="tpu_custom_call" | custom-call | flops 1048576 | bytes 2228224 | tf_op jit(solution)/shard_map/pallas_call | solution.py:44
  96.4 3.4 %all-to-all-start.2 = ((bf16[8,64,256]{2,1,0:T(8,128)(2,1)}), bf16[8,64,256]{2,1,0:T(8,128)(2,1)S(1)}, u32[]{:S(2)}, u32[]{:S(2)}) async-start(bf16[8,64,256]{2,1,0:T(8,128)(2,1)} %bitcast.24), calls=%async_computation.2 | async-start | bytes 524288 | tf_op jit(solution)/shard_map/all_to_all | solution.py:22
  99.8 1.0 constant_dynamic-slice_fusion
  100.8 2.2 %collective-permute-start.13 = (bf16[1024,128]{1,0:T(8,128)(2,1)S(1)}, bf16[1024,128]{1,0:T(8,128)(2,1)S(1)}, u32[]{:S(2)}, u32[]{:S(2)}) collective-permute-start(bf16[1024,128]{1,0:T(8,128)(2,1)S(1)} %bitcast.48), channel_id=1, source_target_pairs={{0,2},{2,0},{1,3},{3,1},{4,6},{6,4},{5,7},{7,5},{8,10},{10,8},{9,1... | collective-permute-start | bytes 786440 | tf_op jit(solution)/shard_map/ppermute | solution.py:30
  102.9 7.4 %all-to-all-done.2 = bf16[8,64,256]{2,1,0:T(8,128)(2,1)S(1)} async-done(((bf16[8,64,256]{2,1,0:T(8,128)(2,1)}), bf16[8,64,256]{2,1,0:T(8,128)(2,1)S(1)}, u32[]{:S(2)}, u32[]{:S(2)}) %all-to-all-start.2) | async-done | bytes 262176 | tf_op jit(solution)/shard_map/all_to_all | solution.py:22
  110.4 0.1 fusion.6
  110.5 0.7 broadcast_in_dim.53
  111.2 3.4 %all-to-all-start.3 = ((bf16[8,64,256]{2,1,0:T(8,128)(2,1)}), bf16[8,64,256]{2,1,0:T(8,128)(2,1)S(1)}, u32[]{:S(2)}, u32[]{:S(2)}) async-start(bf16[8,64,256]{2,1,0:T(8,128)(2,1)} %broadcast_in_dim.53), calls=%async_computation.3 | async-start | bytes 524288 | tf_op jit(solution)/shard_map/all_to_all | solution.py:22
  114.6 0.1 collective-permute-start.12
  114.7 0.0 collective-permute-done.13.refs_2_
  114.7 0.5 collective-permute-start.14
  115.2 1.0 collective-permute-done.12.refs_1_
  116.2 0.4 collective-permute-done.14.refs_3_
  116.6 8.4 %all-to-all-done.3 = bf16[8,64,256]{2,1,0:T(8,128)(2,1)S(1)} async-done(((bf16[8,64,256]{2,1,0:T(8,128)(2,1)}), bf16[8,64,256]{2,1,0:T(8,128)(2,1)S(1)}, u32[]{:S(2)}, u32[]{:S(2)}) %all-to-all-start.3) | async-done | bytes 262176 | tf_op jit(solution)/shard_map/all_to_all | solution.py:22
  125.0 1.8 %shard_map.79 = bf16[8,144,256]{2,1,0:T(8,128)(2,1)S(1)} custom-call(s32[1]{0:T(128)} %bitcast.index_ref, bf16[1024,128]{1,0:T(8,128)(2,1)S(1)} %bitcast.50, bf16[1024,128]{1,0:T(8,128)(2,1)S(1)} %collective-permute-done.12.refs_1_, bf16[1024,128]{1,0:T(8,128)(2,1)S(1)} %collective-permute-done.13.refs_2_, ...), custom_call_target="tpu_custom_call" | custom-call | flops 268435456 | bytes 1572864 | tf_op jit(solution)/shard_map/pallas_call | solution.py:44
  126.8 12.4 %all_to_all.27 = bf16[8,144,256]{2,1,0:T(8,128)(2,1)S(1)} all-to-all(bf16[8,144,256]{2,1,0:T(8,128)(2,1)S(1)} %shard_map.79), channel_id=1, replica_groups=mesh['z'=8,'x'=4,'yl'=2,'yh'=2,'core'=2] {'x','yl'}, dimensions={0} | all-to-all | bytes 1179648 | tf_op jit(solution)/shard_map/all_to_all | solution.py:22
  139.3 0.3 copy.26
  139.6 1.0 copy.27
  140.6 0.7 fusion.5
  (17 shorter events, 0.5 us)
Async XLA Ops:
  24.9 8.7 %collective-permute-start.1 = (bf16[8,128,128]{2,1,0:T(8,128)(2,1)S(1)}, bf16[8,128,128]{2,1,0:T(8,128)(2,1)S(1)}, u32[]{:S(2)}, u32[]{:S(2)}) collective-permute-start(bf16[8,128,128]{2,1,0:T(8,128)(2,1)S(1)} %bitcast.56), channel_id=1, source_target_pairs={{0,8},{8,16},{16,24},{24,0},{1,9},{9,17},{17,25},{25,1},{2,10},{10... | collective-permute-start | bytes 786440 | tf_op jit(solution)/shard_map/ppermute | solution.py:60
  26.4 7.6 %collective-permute-start.2 = (bf16[8,128,128]{2,1,0:T(8,128)(2,1)S(1)}, bf16[8,128,128]{2,1,0:T(8,128)(2,1)S(1)}, u32[]{:S(2)}, u32[]{:S(2)}) collective-permute-start(bf16[8,128,128]{2,1,0:T(8,128)(2,1)S(1)} %bitcast.57), channel_id=1, source_target_pairs={{0,24},{8,0},{16,8},{24,16},{1,25},{9,1},{17,9},{25,17},{2,26},{10... | collective-permute-start | bytes 786440 | tf_op jit(solution)/shard_map/ppermute | solution.py:60
  28.2 8.9 %collective-permute-start = (bf16[8,128,128]{2,1,0:T(8,128)(2,1)S(1)}, bf16[8,128,128]{2,1,0:T(8,128)(2,1)S(1)}, u32[]{:S(2)}, u32[]{:S(2)}) collective-permute-start(bf16[8,128,128]{2,1,0:T(8,128)(2,1)S(1)} %bitcast.58), channel_id=1, source_target_pairs={{0,4},{4,0},{1,5},{5,1},{2,6},{6,2},{3,7},{7,3},{8,12},{12,8},{9,1... | collective-permute-start | bytes 786440 | tf_op jit(solution)/shard_map/ppermute | solution.py:30
  33.7 10.3 %collective-permute-start.3 = (bf16[4,128,128]{2,1,0:T(8,128)(2,1)S(1)}, bf16[4,128,128]{2,1,0:T(8,128)(2,1)S(1)}, u32[]{:S(2)}, u32[]{:S(2)}) collective-permute-start(bf16[4,128,128]{2,1,0:T(8,128)(2,1)S(1)} %slice.26), channel_id=1, source_target_pairs={{0,8},{8,16},{16,24},{24,0},{1,9},{9,17},{17,25},{25,1},{2,10},{10... | collective-permute-start | bytes 393224 | tf_op jit(solution)/shard_map/ppermute | solution.py:60
  34.1 11.3 %collective-permute-start.4 = (bf16[4,128,128]{2,1,0:T(8,128)(2,1)S(1)}, bf16[4,128,128]{2,1,0:T(8,128)(2,1)S(1)}, u32[]{:S(2)}, u32[]{:S(2)}) collective-permute-start(bf16[4,128,128]{2,1,0:T(8,128)(2,1)S(1)} %slice.27), channel_id=1, source_target_pairs={{0,24},{8,0},{16,8},{24,16},{1,25},{9,1},{17,9},{25,17},{2,26},{10... | collective-permute-start | bytes 393224 | tf_op jit(solution)/shard_map/ppermute | solution.py:60
  40.5 7.7 %collective-permute-start.5 = (bf16[8,128,128]{2,1,0:T(8,128)(2,1)S(1)}, bf16[8,128,128]{2,1,0:T(8,128)(2,1)S(1)}, u32[]{:S(2)}, u32[]{:S(2)}) collective-permute-start(bf16[8,128,128]{2,1,0:T(8,128)(2,1)S(1)} %collective-permute-done), channel_id=1, source_target_pairs={{0,8},{8,16},{16,24},{24,0},{1,9},{9,17},{17,25},{25,1},{2,10},{10... | collective-permute-start | bytes 786440 | tf_op jit(solution)/shard_map/ppermute | solution.py:60
  40.6 7.6 %collective-permute-start.6 = (bf16[8,128,128]{2,1,0:T(8,128)(2,1)S(1)}, bf16[8,128,128]{2,1,0:T(8,128)(2,1)S(1)}, u32[]{:S(2)}, u32[]{:S(2)}) collective-permute-start(bf16[8,128,128]{2,1,0:T(8,128)(2,1)S(1)} %collective-permute-done), channel_id=1, source_target_pairs={{0,24},{8,0},{16,8},{24,16},{1,25},{9,1},{17,9},{25,17},{2,26},{10... | collective-permute-start | bytes 786440 | tf_op jit(solution)/shard_map/ppermute | solution.py:60
  44.0 5.1 %collective-permute-start.7 = (bf16[4,128,128]{2,1,0:T(8,128)(2,1)S(1)}, bf16[4,128,128]{2,1,0:T(8,128)(2,1)S(1)}, u32[]{:S(2)}, u32[]{:S(2)}) collective-permute-start(bf16[4,128,128]{2,1,0:T(8,128)(2,1)S(1)} %collective-permute-done.3), channel_id=1, source_target_pairs={{0,4},{4,0},{1,5},{5,1},{2,6},{6,2},{3,7},{7,3},{8,12},{12,8},{9,1... | collective-permute-start | bytes 393224 | tf_op jit(solution)/shard_map/ppermute | solution.py:30
  45.3 5.1 %collective-permute-start.8 = (bf16[4,128,128]{2,1,0:T(8,128)(2,1)S(1)}, bf16[4,128,128]{2,1,0:T(8,128)(2,1)S(1)}, u32[]{:S(2)}, u32[]{:S(2)}) collective-permute-start(bf16[4,128,128]{2,1,0:T(8,128)(2,1)S(1)} %collective-permute-done.4), channel_id=1, source_target_pairs={{0,4},{4,0},{1,5},{5,1},{2,6},{6,2},{3,7},{7,3},{8,12},{12,8},{9,1... | collective-permute-start | bytes 393224 | tf_op jit(solution)/shard_map/ppermute | solution.py:30
  50.4 3.0 %copy-start.3 = (bf16[8,8,128,128]{3,2,1,0:T(8,128)(2,1)}, bf16[8,8,128,128]{3,2,1,0:T(8,128)(2,1)S(1)}, u32[]{:S(2)}) copy-start(bf16[8,8,128,128]{3,2,1,0:T(8,128)(2,1)S(1)} %bitcast_dynamic-update-slice_fusion.8) | copy-start | bytes 6291460
  50.4 10.9 %copy-start = (bf16[512,2048]{1,0:T(8,128)(2,1)S(1)}, bf16[512,2048]{1,0:T(8,128)(2,1)}, u32[]{:S(2)}) copy-start(bf16[512,2048]{1,0:T(8,128)(2,1)} %refs_4_.1) | copy-start | bytes 6291460
  50.5 10.9 %copy-start.1 = (f32[8,2048]{1,0:T(8,128)S(1)}, f32[8,2048]{1,0:T(8,128)}, u32[]{:S(2)}) copy-start(f32[8,2048]{1,0:T(8,128)} %refs_5_.1) | copy-start | bytes 196612
  50.5 10.8 %copy-start.2 = (f32[8,2048]{1,0:T(8,128)S(1)}, f32[8,2048]{1,0:T(8,128)}, u32[]{:S(2)}) copy-start(f32[8,2048]{1,0:T(8,128)} %refs_6_.1) | copy-start | bytes 196612
  53.4 6.6 %collective-permute-start.10 = (bf16[128,512]{1,0:T(8,128)(2,1)S(1)}, bf16[128,512]{1,0:T(8,128)(2,1)S(1)}, u32[]{:S(2)}, u32[]{:S(2)}) collective-permute-start(bf16[128,512]{1,0:T(8,128)(2,1)S(1)} %convolution_convert_fusion.refs_0_), channel_id=1, source_target_pairs={{0,2},{2,0},{1,3},{3,1},{4,6},{6,4},{5,7},{7,5},{8,10},{10,8},{9,1... | collective-permute-start | bytes 393224 | tf_op jit(solution)/shard_map/ppermute | solution.py:30
  55.5 4.4 %collective-permute-start.9 = (bf16[128,512]{1,0:T(8,128)(2,1)S(1)}, bf16[128,512]{1,0:T(8,128)(2,1)S(1)}, u32[]{:S(2)}, u32[]{:S(2)}) collective-permute-start(bf16[128,512]{1,0:T(8,128)(2,1)S(1)} %convolution_convert_fusion.refs_0_), channel_id=1, source_target_pairs={{0,1},{1,0},{2,3},{3,2},{4,5},{5,4},{6,7},{7,6},{8,9},{9,8},{10,11... | collective-permute-start | bytes 393224 | tf_op jit(solution)/shard_map/ppermute | solution.py:30
  60.0 1.3 collective-permute-start.11
  96.4 14.0 %all-to-all-start.2 = ((bf16[8,64,256]{2,1,0:T(8,128)(2,1)}), bf16[8,64,256]{2,1,0:T(8,128)(2,1)S(1)}, u32[]{:S(2)}, u32[]{:S(2)}) async-start(bf16[8,64,256]{2,1,0:T(8,128)(2,1)} %bitcast.24), calls=%async_computation.2 | async-start | bytes 524288 | tf_op jit(solution)/shard_map/all_to_all | solution.py:22
  100.8 13.9 %collective-permute-start.13 = (bf16[1024,128]{1,0:T(8,128)(2,1)S(1)}, bf16[1024,128]{1,0:T(8,128)(2,1)S(1)}, u32[]{:S(2)}, u32[]{:S(2)}) collective-permute-start(bf16[1024,128]{1,0:T(8,128)(2,1)S(1)} %bitcast.48), channel_id=1, source_target_pairs={{0,2},{2,0},{1,3},{3,1},{4,6},{6,4},{5,7},{7,5},{8,10},{10,8},{9,1... | collective-permute-start | bytes 786440 | tf_op jit(solution)/shard_map/ppermute | solution.py:30
  111.2 13.8 %all-to-all-start.3 = ((bf16[8,64,256]{2,1,0:T(8,128)(2,1)}), bf16[8,64,256]{2,1,0:T(8,128)(2,1)S(1)}, u32[]{:S(2)}, u32[]{:S(2)}) async-start(bf16[8,64,256]{2,1,0:T(8,128)(2,1)} %broadcast_in_dim.53), calls=%async_computation.3 | async-start | bytes 524288 | tf_op jit(solution)/shard_map/all_to_all | solution.py:22
  114.6 1.6 %collective-permute-start.12 = (bf16[1024,128]{1,0:T(8,128)(2,1)S(1)}, bf16[1024,128]{1,0:T(8,128)(2,1)S(1)}, u32[]{:S(2)}, u32[]{:S(2)}) collective-permute-start(bf16[1024,128]{1,0:T(8,128)(2,1)S(1)} %bitcast.49), channel_id=1, source_target_pairs={{0,1},{1,0},{2,3},{3,2},{4,5},{5,4},{6,7},{7,6},{8,9},{9,8},{10,11... | collective-permute-start | bytes 786440 | tf_op jit(solution)/shard_map/ppermute | solution.py:30
  114.7 1.9 %collective-permute-start.14 = (bf16[1024,128]{1,0:T(8,128)(2,1)S(1)}, bf16[1024,128]{1,0:T(8,128)(2,1)S(1)}, u32[]{:S(2)}, u32[]{:S(2)}) collective-permute-start(bf16[1024,128]{1,0:T(8,128)(2,1)S(1)} %collective-permute-done.13.refs_2_), channel_id=1, source_target_pairs={{0,1},{1,0},{2,3},{3,2},{4,5},{5,4},{6,7},{7,6},{8,9},{9,8},{10,11... | collective-permute-start | bytes 786440 | tf_op jit(solution)/shard_map/ppermute | solution.py:30

commit v5 on v4

--- a/solution.py
+++ b/solution.py
@@ -82,7 +82,7 @@
     for piece, dx, dy, start in pieces:
         member = ((x + dx) & (NX - 1)) * NYL + (yl ^ dy)
         blocks = lax.dynamic_update_slice(blocks, piece[:, None], (start, member, 0, 0))
-    return blocks, beside
+    return blocks
 
 
 def loaded(*arrays):
@@ -211,19 +211,20 @@
             total += jnp.dot(
                 blocks[k][...], step_ref[pl.ds(start, quarter), :], preferred_element_type=F32
             )
-        out[0, :group, :] = total.astype(BF16)
-        out[0, group:, :] = jnp.concatenate(halves(projected_ref[...]))
+        for j in range(PAIR):
+            out[j, :group, :] = total[j * group : (j + 1) * group].astype(BF16)
+            out[j, group:, :] = jnp.concatenate(halves(projected_ref[j * own : (j + 1) * own, :]))
 
     return call(
         kernel,
         index,
-        (NP,),
-        [pl.BlockSpec((group, quarter), lambda p, t: (p, 0))] * NT
+        (NP // PAIR,),
+        [pl.BlockSpec((PAIR * group, quarter), lambda p, t: (p, 0))] * NT
         + [
             pl.BlockSpec((NT * quarter, part), lambda p, t: (0, 0)),
-            pl.BlockSpec((own, part), lambda p, t: (p, 0)),
-        ],
-        pl.BlockSpec((1, group + 2 * own, part), lambda p, t: (p, 0, 0)),
+            pl.BlockSpec((PAIR * own, part), lambda p, t: (p, 0)),
+        ],
+        pl.BlockSpec((PAIR, group + 2 * own, part), lambda p, t: (p, 0, 0)),
         jax.ShapeDtypeStruct((NP, group + 2 * own, part), BF16),
         [],
         (2 * NP * group * NT * quarter * part, 2 * NP * group * (NT * quarter + part)),
@@ -231,6 +232,42 @@
         *pieces,
         step_dir,
         projected,
+    )
+
+
+def outputs(index, back, first_moment, second_moment):
+    own, columns = first_moment.shape
+    members, rows, part = back.shape
+    group, count = rows - 2 * own, members // 2
+    wide = count * part
+
+    def kernel(index_ref, back_ref, first_ref, second_ref, update, new_first, new_second):
+        for j in range(count):
+            here = slice(j * part, (j + 1) * part)
+            update[:, here] = back_ref[j, :group, :]
+            terms = back_ref[j, group:, :].astype(F32)
+            new_first[:, here], new_second[:, here] = moments_of(
+                first_ref[:, here], second_ref[:, here], terms[:own] + terms[own:]
+            )
+
+    moment = pl.BlockSpec((own, wide), lambda p, t: (0, p))
+    return call(
+        kernel,
+        index,
+        (2,),
+        [pl.BlockSpec((count, rows, part), lambda p, t: (p, 0, 0)), moment, moment],
+        [pl.BlockSpec((group, wide), lambda p, t: (0, p)), moment, moment],
+        [
+            jax.ShapeDtypeStruct((group, columns), BF16),
+            jax.ShapeDtypeStruct((own, columns), F32),
+            jax.ShapeDtypeStruct((own, columns), F32),
+        ],
+        [],
+        (8 * own * columns, 4 * columns * (rows + 4 * own)),
+        16,
+        back,
+        first_moment,
+        second_moment,
     )
 
 
@@ -252,8 +289,8 @@
     pieces = basis.reshape(rows, NT, quarter).transpose(1, 0, 2)
     pieces = jnp.broadcast_to(pieces[None], (NZ, NT, rows, quarter))
     line = exchange(pieces.reshape(NZ * NT, rows, quarter), ("z",) + TENSOR)
-    blocks, beside = plane_blocks(line.reshape(NZ, group, quarter))
-    tokens, beside = lax.optimization_barrier((tokens, beside))
+    tokens, line = lax.optimization_barrier((tokens, line))
+    blocks = plane_blocks(line.reshape(NZ, group, quarter))
     (tokens,) = loaded(tokens)
     coords = peers(coordinates(tokens, blocks))
 
@@ -273,10 +310,10 @@
     step_dir = gather(step_dir, ("z",), NZ).reshape(rank, part)
 
     back = update_blocks(index, rows_here, step_dir, projected, own)
-    back = exchange(back, PLANE).transpose(1, 0, 2).reshape(group + 2 * own, columns)
-    projected = back[group : group + own].astype(F32) + back[group + own :].astype(F32)
-    new_first, new_second = moments_of(first_moment, second_moment, projected)
-    return (back[:group], new_first, new_second)
+    update, new_first, new_second = outputs(
+        index, exchange(back, PLANE), first_moment, second_moment
+    )
+    return (update, new_first, new_second)
 
 
 def solution(mesh):

time: 143 us -> 138 us (0.965)
  starting transfers between devices: 25 us -> 23 us
    ppermute x6, waiting for transfers between devices: 5.7 us -> 3.28 us  [along(): return lax.ppermute(block, 'x', [(i, (i + shift) % NX) for i in range(NX)])]
    ppermute x9, starting transfers between devices: 8.27 us -> 6.32 us  [swap(): return lax.ppermute(block, axis, ((0, 1), (1, 0)))]
    all_to_all x2, waiting for transfers between devices: 15.8 us -> 17.4 us  [exchange(): return lax.all_to_all(blocks, axes, 0, 0, tiled=True)]
    pallas_call x3 -> x4, Pallas kernels: 5.5 us -> 5.73 us  [call(): pl.pallas_call(kernel, grid_spec=pltpu.PrefetchScalarGridSpec(num_scalar_...]
  transfers between devices with their start and end apart: 17 -> 17, of which waited for: 10 -> 11; matrix products, arithmetic and copies ran while one was open for 2% -> 2% of each run, Pallas kernels for 2% -> 2%
where the time goes in v5:
time: 138 us
  blocking collectives  68 us (49%)
  waiting for transfers between devices  30.3 us (22%)
  starting transfers between devices  23 us (17%)
  Pallas kernels  9.11 us (7%)
  local copies, waits for them, and re-layouts  3.36 us (2%)
  matrix products  2.92 us (2%)
    all_to_all x3, blocking collectives, exchange(): return lax.all_to_all(blocks, axes, 0, 0, tiled=True)  68 us
    all_to_all x2, waiting for transfers between devices, exchange(): return lax.all_to_all(blocks, axes, 0, 0, tiled=True)  17.4 us
    ppermute x6, starting transfers between devices, along(): return lax.ppermute(block, 'x', [(i, (i + shift) % NX) for i in range(NX)])  9.86 us
    ppermute x9, waiting for transfers between devices, swap(): return lax.ppermute(block, axis, ((0, 1), (1, 0)))  9.58 us
    all_to_all x2, starting transfers between devices, exchange(): return lax.all_to_all(blocks, axes, 0, 0, tiled=True)  6.83 us
    ppermute x9, starting transfers between devices, swap(): return lax.ppermute(block, axis, ((0, 1), (1, 0)))  6.32 us
    pallas_call x4, Pallas kernels, call(): pl.pallas_call(kernel, grid_spec=pltpu.PrefetchScalarGridSpec(num_scalar_...  5.73 us
    pallas_call x1, Pallas kernels, loaded(): pl.pallas_call(kernel, in_specs=[pl.BlockSpec(memory_space=pltpu.HBM)] *...  3.39 us
  transfers between devices with their start and end apart: 17, of which 11 were waited for; matrix products, arithmetic and copies ran while one was open for 2% of the time, Pallas kernels for 2%

profile of v5, /device:TPU:16, one launch (start us, length us, event | category | flops | bytes accessed | tf_op | source)
XLA Modules:
  0.0 137.7 jit_solution(8379683686714372561)
XLA Ops:
  0.6 0.8 reshape.34
  1.5 23.5 %all_to_all.25 = bf16[32,32,128]{2,1,0:T(8,128)(2,1)S(1)} all-to-all(bf16[32,32,128]{2,1,0:T(8,128)(2,1)S(1)} %bitcast.54), channel_id=1, replica_groups=mesh['z'=8,'x'=4,'yl'=2,'yh'=2,'core'=2] {'z','yh','core'}, dimensions={0} | all-to-all | bytes 524288 | tf_op jit(solution)/shard_map/all_to_all | solution.py:22
  24.9 1.5 %collective-permute-start.1 = (bf16[8,128,128]{2,1,0:T(8,128)(2,1)S(1)}, bf16[8,128,128]{2,1,0:T(8,128)(2,1)S(1)}, u32[]{:S(2)}, u32[]{:S(2)}) collective-permute-start(bf16[8,128,128]{2,1,0:T(8,128)(2,1)S(1)} %bitcast.50), channel_id=1, source_target_pairs={{0,8},{8,16},{16,24},{24,0},{1,9},{9,17},{17,25},{25,1},{2,10},{10... | collective-permute-start | bytes 786440 | tf_op jit(solution)/shard_map/ppermute | solution.py:60
  26.4 1.7 %collective-permute-start.2 = (bf16[8,128,128]{2,1,0:T(8,128)(2,1)S(1)}, bf16[8,128,128]{2,1,0:T(8,128)(2,1)S(1)}, u32[]{:S(2)}, u32[]{:S(2)}) collective-permute-start(bf16[8,128,128]{2,1,0:T(8,128)(2,1)S(1)} %bitcast.51), channel_id=1, source_target_pairs={{0,24},{8,0},{16,8},{24,16},{1,25},{9,1},{17,9},{25,17},{2,26},{10... | collective-permute-start | bytes 786440 | tf_op jit(solution)/shard_map/ppermute | solution.py:60
  28.2 1.3 collective-permute-start
  29.5 3.4 %shard_map.76 = bf16[512,8192]{1,0:T(8,128)(2,1)S(1)} custom-call(bf16[512,8192]{1,0:T(8,128)(2,1)} %refs_0_), custom_call_target="tpu_custom_call" | custom-call | bytes 16777216 | tf_op jit(solution)/shard_map/pallas_call | solution.py:101
  32.9 0.5 broadcast_in_dim.42
  33.4 0.3 collective-permute-done.1
  33.7 0.4 collective-permute-start.3
  34.0 0.0 collective-permute-done.2
  34.1 3.0 %collective-permute-start.4 = (bf16[4,128,128]{2,1,0:T(8,128)(2,1)S(1)}, bf16[4,128,128]{2,1,0:T(8,128)(2,1)S(1)}, u32[]{:S(2)}, u32[]{:S(2)}) collective-permute-start(bf16[4,128,128]{2,1,0:T(8,128)(2,1)S(1)} %slice.9), channel_id=1, source_target_pairs={{0,24},{8,0},{16,8},{24,16},{1,25},{9,1},{17,9},{25,17},{2,26},{10... | collective-permute-start | bytes 393224 | tf_op jit(solution)/shard_map/ppermute | solution.py:60
  37.1 0.0 collective-permute-done
  37.1 0.0 collective-permute-start.5
  37.1 3.2 %collective-permute-start.6 = (bf16[8,128,128]{2,1,0:T(8,128)(2,1)S(1)}, bf16[8,128,128]{2,1,0:T(8,128)(2,1)S(1)}, u32[]{:S(2)}, u32[]{:S(2)}) collective-permute-start(bf16[8,128,128]{2,1,0:T(8,128)(2,1)S(1)} %collective-permute-done), channel_id=1, source_target_pairs={{0,24},{8,0},{16,8},{24,16},{1,25},{9,1},{17,9},{25,17},{2,26},{10... | collective-permute-start | bytes 786440 | tf_op jit(solution)/shard_map/ppermute | solution.py:60
  40.5 0.7 collective-permute-done.3
  41.1 1.3 collective-permute-start.7
  42.4 0.0 collective-permute-done.4
  42.4 0.7 collective-permute-start.8
  43.2 2.3 %collective-permute-done.5 = bf16[8,128,128]{2,1,0:T(8,128)(2,1)S(1)} collective-permute-done((bf16[8,128,128]{2,1,0:T(8,128)(2,1)S(1)}, bf16[8,128,128]{2,1,0:T(8,128)(2,1)S(1)}, u32[]{:S(2)}, u32[]{:S(2)}) %collective-permute-start.5) | collective-permute-done | bytes 262176 | tf_op jit(solution)/shard_map/ppermute | solution.py:60
  45.6 0.0 collective-permute-done.6
  45.7 0.5 collective-permute-done.7
  46.1 1.4 %collective-permute-done.8 = bf16[4,128,128]{2,1,0:T(8,128)(2,1)S(1)} collective-permute-done((bf16[4,128,128]{2,1,0:T(8,128)(2,1)S(1)}, bf16[4,128,128]{2,1,0:T(8,128)(2,1)S(1)}, u32[]{:S(2)}, u32[]{:S(2)}) %collective-permute-start.8) | collective-permute-done | bytes 131104 | tf_op jit(solution)/shard_map/ppermute | solution.py:30
  47.5 0.0 copy-start.3
  47.5 0.0 copy-start
  47.6 0.0 copy-start.1
  47.6 0.0 copy-start.2
  47.6 2.9 %convolution_convert_fusion.refs_0_ = bf16[128,512]{1,0:T(8,128)(2,1)S(1)} fusion(bf16[8192,128]{1,0:T(8,128)(2,1)S(1)} %bitcast.49, bf16[512,8192]{1,0:T(8,128)(2,1)S(1)} %shard_map.76), kind=kOutput, calls=%fused_computation | convolution fusion | flops 1073807360 | bytes 10616832 | tf_op jit(solution)/shard_map/dot_general | solution.py:116
  50.5 0.0 copy-done.3
  50.5 1.6 %collective-permute-start.10 = (bf16[128,512]{1,0:T(8,128)(2,1)S(1)}, bf16[128,512]{1,0:T(8,128)(2,1)S(1)}, u32[]{:S(2)}, u32[]{:S(2)}) collective-permute-start(bf16[128,512]{1,0:T(8,128)(2,1)S(1)} %convolution_convert_fusion.refs_0_), channel_id=1, source_target_pairs={{0,2},{2,0},{1,3},{3,1},{4,6},{6,4},{5,7},{7,5},{8,10},{10,8},{9,1... | collective-permute-start | bytes 393224 | tf_op jit(solution)/shard_map/ppermute | solution.py:30
  52.1 0.0 collective-permute-start.9
  52.1 5.0 %collective-permute-done.10.refs_2_ = bf16[128,512]{1,0:T(8,128)(2,1)S(1)} collective-permute-done((bf16[128,512]{1,0:T(8,128)(2,1)S(1)}, bf16[128,512]{1,0:T(8,128)(2,1)S(1)}, u32[]{:S(2)}, u32[]{:S(2)}) %collective-permute-start.10) | collective-permute-done | bytes 131104 | tf_op jit(solution)/shard_map/ppermute | solution.py:30
  57.1 0.0 collective-permute-start.11
  57.1 0.0 collective-permute-done.9.refs_1_
  57.1 1.3 collective-permute-done.11.refs_3_
  58.4 0.0 copy-done
  58.4 0.0 copy-done.1
  58.4 0.0 copy-done.2
  58.4 2.0 %shard_map.77 = bf16[8,544,256]{2,1,0:T(8,128)(2,1)S(1)} custom-call(s32[1]{0:T(128)} %bitcast.index_ref, bf16[128,512]{1,0:T(8,128)(2,1)S(1)} %convolution_convert_fusion.refs_0_, bf16[128,512]{1,0:T(8,128)(2,1)S(1)} %collective-permute-done.9.refs_1_, bf16[128,512]{1,0:T(8,128)(2,1)S(1)} %collective-permute-done.10.refs_2_, ...), custom_call_target="tpu_custom_call" | custom-call | flops 1073741824 | bytes 4325376 | tf_op jit(solution)/shard_map/pallas_call | solution.py:44
  60.5 32.4 %all_to_all.26.sums_ref.moments_ref = bf16[8,544,256]{2,1,0:T(8,128)(2,1)S(1)} all-to-all(bf16[8,544,256]{2,1,0:T(8,128)(2,1)S(1)} %shard_map.77), channel_id=1, replica_groups=mesh['z'=8,'x'=4,'yl'=2,'yh'=2,'core'=2] {'x','yl'}, dimensions={0} | all-to-all | bytes 4456448 | tf_op jit(solution)/shard_map/all_to_all | solution.py:22
  92.9 1.7 %shard_map.78 = (bf16[512,256]{1,0:T(8,128)(2,1)}, f32[64,256]{1,0:T(8,128)S(1)}, f32[64,256]{1,0:T(8,128)S(1)}) custom-call(s32[1]{0:T(128)} %bitcast.index_ref, bf16[8,544,256]{2,1,0:T(8,128)(2,1)S(1)} %all_to_all.26.sums_ref.moments_ref, bf16[8,544,256]{2,1,0:T(8,128)(2,1)S(1)} %all_to_all.26.sums_ref.moments_ref), custom_call_target="tpu_custom_call" | custom-call | flops 1048576 | bytes 2228224 | tf_op jit(solution)/shard_map/pallas_call | solution.py:44
  94.6 3.4 %all-to-all-start.2 = ((bf16[8,64,256]{2,1,0:T(8,128)(2,1)}), bf16[8,64,256]{2,1,0:T(8,128)(2,1)S(1)}, u32[]{:S(2)}, u32[]{:S(2)}) async-start(bf16[8,64,256]{2,1,0:T(8,128)(2,1)} %bitcast.24), calls=%async_computation.2 | async-start | bytes 524288 | tf_op jit(solution)/shard_map/all_to_all | solution.py:22
  98.0 1.0 constant_dynamic-slice_fusion
  99.0 0.9 collective-permute-start.13
  99.8 9.0 %all-to-all-done.2 = bf16[8,64,256]{2,1,0:T(8,128)(2,1)S(1)} async-done(((bf16[8,64,256]{2,1,0:T(8,128)(2,1)}), bf16[8,64,256]{2,1,0:T(8,128)(2,1)S(1)}, u32[]{:S(2)}, u32[]{:S(2)}) %all-to-all-start.2) | async-done | bytes 262176 | tf_op jit(solution)/shard_map/all_to_all | solution.py:22
  108.9 0.1 fusion.5
  109.0 0.7 broadcast_in_dim.53
  109.7 3.4 %all-to-all-start.3 = ((bf16[8,64,256]{2,1,0:T(8,128)(2,1)}), bf16[8,64,256]{2,1,0:T(8,128)(2,1)S(1)}, u32[]{:S(2)}, u32[]{:S(2)}) async-start(bf16[8,64,256]{2,1,0:T(8,128)(2,1)} %broadcast_in_dim.53), calls=%async_computation.3 | async-start | bytes 524288 | tf_op jit(solution)/shard_map/all_to_all | solution.py:22
  113.1 0.1 collective-permute-start.12
  113.2 0.0 collective-permute-done.13.refs_2_
  113.2 0.5 collective-permute-start.14
  113.7 1.0 collective-permute-done.12.refs_1_
  114.7 0.4 collective-permute-done.14.refs_3_
  115.1 8.4 %all-to-all-done.3 = bf16[8,64,256]{2,1,0:T(8,128)(2,1)S(1)} async-done(((bf16[8,64,256]{2,1,0:T(8,128)(2,1)}), bf16[8,64,256]{2,1,0:T(8,128)(2,1)S(1)}, u32[]{:S(2)}, u32[]{:S(2)}) %all-to-all-start.3) | async-done | bytes 262176 | tf_op jit(solution)/shard_map/all_to_all | solution.py:22
  123.5 1.2 shard_map.79
  124.7 12.1 %all_to_all.27.back_ref = bf16[8,144,256]{2,1,0:T(8,128)(2,1)S(1)} all-to-all(bf16[8,144,256]{2,1,0:T(8,128)(2,1)S(1)} %shard_map.79), channel_id=1, replica_groups=mesh['z'=8,'x'=4,'yl'=2,'yh'=2,'core'=2] {'x','yl'}, dimensions={0} | all-to-all | bytes 1179648 | tf_op jit(solution)/shard_map/all_to_all | solution.py:22
  136.8 0.8 shard_map.80
  (15 shorter events, 0.4 us)
Async XLA Ops:
  24.9 8.7 %collective-permute-start.1 = (bf16[8,128,128]{2,1,0:T(8,128)(2,1)S(1)}, bf16[8,128,128]{2,1,0:T(8,128)(2,1)S(1)}, u32[]{:S(2)}, u32[]{:S(2)}) collective-permute-start(bf16[8,128,128]{2,1,0:T(8,128)(2,1)S(1)} %bitcast.50), channel_id=1, source_target_pairs={{0,8},{8,16},{16,24},{24,0},{1,9},{9,17},{17,25},{25,1},{2,10},{10... | collective-permute-start | bytes 786440 | tf_op jit(solution)/shard_map/ppermute | solution.py:60
  26.4 7.6 %collective-permute-start.2 = (bf16[8,128,128]{2,1,0:T(8,128)(2,1)S(1)}, bf16[8,128,128]{2,1,0:T(8,128)(2,1)S(1)}, u32[]{:S(2)}, u32[]{:S(2)}) collective-permute-start(bf16[8,128,128]{2,1,0:T(8,128)(2,1)S(1)} %bitcast.51), channel_id=1, source_target_pairs={{0,24},{8,0},{16,8},{24,16},{1,25},{9,1},{17,9},{25,17},{2,26},{10... | collective-permute-start | bytes 786440 | tf_op jit(solution)/shard_map/ppermute | solution.py:60
  28.2 8.9 %collective-permute-start = (bf16[8,128,128]{2,1,0:T(8,128)(2,1)S(1)}, bf16[8,128,128]{2,1,0:T(8,128)(2,1)S(1)}, u32[]{:S(2)}, u32[]{:S(2)}) collective-permute-start(bf16[8,128,128]{2,1,0:T(8,128)(2,1)S(1)} %bitcast.52), channel_id=1, source_target_pairs={{0,4},{4,0},{1,5},{5,1},{2,6},{6,2},{3,7},{7,3},{8,12},{12,8},{9,1... | collective-permute-start | bytes 786440 | tf_op jit(solution)/shard_map/ppermute | solution.py:30
  33.7 7.5 %collective-permute-start.3 = (bf16[4,128,128]{2,1,0:T(8,128)(2,1)S(1)}, bf16[4,128,128]{2,1,0:T(8,128)(2,1)S(1)}, u32[]{:S(2)}, u32[]{:S(2)}) collective-permute-start(bf16[4,128,128]{2,1,0:T(8,128)(2,1)S(1)} %slice.8), channel_id=1, source_target_pairs={{0,8},{8,16},{16,24},{24,0},{1,9},{9,17},{17,25},{25,1},{2,10},{10... | collective-permute-start | bytes 393224 | tf_op jit(solution)/shard_map/ppermute | solution.py:60
  34.1 8.4 %collective-permute-start.4 = (bf16[4,128,128]{2,1,0:T(8,128)(2,1)S(1)}, bf16[4,128,128]{2,1,0:T(8,128)(2,1)S(1)}, u32[]{:S(2)}, u32[]{:S(2)}) collective-permute-start(bf16[4,128,128]{2,1,0:T(8,128)(2,1)S(1)} %slice.9), channel_id=1, source_target_pairs={{0,24},{8,0},{16,8},{24,16},{1,25},{9,1},{17,9},{25,17},{2,26},{10... | collective-permute-start | bytes 393224 | tf_op jit(solution)/shard_map/ppermute | solution.py:60
  37.1 8.5 %collective-permute-start.5 = (bf16[8,128,128]{2,1,0:T(8,128)(2,1)S(1)}, bf16[8,128,128]{2,1,0:T(8,128)(2,1)S(1)}, u32[]{:S(2)}, u32[]{:S(2)}) collective-permute-start(bf16[8,128,128]{2,1,0:T(8,128)(2,1)S(1)} %collective-permute-done), channel_id=1, source_target_pairs={{0,8},{8,16},{16,24},{24,0},{1,9},{9,17},{17,25},{25,1},{2,10},{10... | collective-permute-start | bytes 786440 | tf_op jit(solution)/shard_map/ppermute | solution.py:60
  37.1 8.5 %collective-permute-start.6 = (bf16[8,128,128]{2,1,0:T(8,128)(2,1)S(1)}, bf16[8,128,128]{2,1,0:T(8,128)(2,1)S(1)}, u32[]{:S(2)}, u32[]{:S(2)}) collective-permute-start(bf16[8,128,128]{2,1,0:T(8,128)(2,1)S(1)} %collective-permute-done), channel_id=1, source_target_pairs={{0,24},{8,0},{16,8},{24,16},{1,25},{9,1},{17,9},{25,17},{2,26},{10... | collective-permute-start | bytes 786440 | tf_op jit(solution)/shard_map/ppermute | solution.py:60
  41.1 5.0 %collective-permute-start.7 = (bf16[4,128,128]{2,1,0:T(8,128)(2,1)S(1)}, bf16[4,128,128]{2,1,0:T(8,128)(2,1)S(1)}, u32[]{:S(2)}, u32[]{:S(2)}) collective-permute-start(bf16[4,128,128]{2,1,0:T(8,128)(2,1)S(1)} %collective-permute-done.3), channel_id=1, source_target_pairs={{0,4},{4,0},{1,5},{5,1},{2,6},{6,2},{3,7},{7,3},{8,12},{12,8},{9,1... | collective-permute-start | bytes 393224 | tf_op jit(solution)/shard_map/ppermute | solution.py:30
  42.4 5.1 %collective-permute-start.8 = (bf16[4,128,128]{2,1,0:T(8,128)(2,1)S(1)}, bf16[4,128,128]{2,1,0:T(8,128)(2,1)S(1)}, u32[]{:S(2)}, u32[]{:S(2)}) collective-permute-start(bf16[4,128,128]{2,1,0:T(8,128)(2,1)S(1)} %collective-permute-done.4), channel_id=1, source_target_pairs={{0,4},{4,0},{1,5},{5,1},{2,6},{6,2},{3,7},{7,3},{8,12},{12,8},{9,1... | collective-permute-start | bytes 393224 | tf_op jit(solution)/shard_map/ppermute | solution.py:30
  47.5 3.0 %copy-start.3 = (bf16[8,8,128,128]{3,2,1,0:T(8,128)(2,1)}, bf16[8,8,128,128]{3,2,1,0:T(8,128)(2,1)S(1)}, u32[]{:S(2)}) copy-start(bf16[8,8,128,128]{3,2,1,0:T(8,128)(2,1)S(1)} %bitcast_dynamic-update-slice_fusion.8) | copy-start | bytes 6291460
  47.5 10.9 %copy-start = (bf16[512,2048]{1,0:T(8,128)(2,1)S(1)}, bf16[512,2048]{1,0:T(8,128)(2,1)}, u32[]{:S(2)}) copy-start(bf16[512,2048]{1,0:T(8,128)(2,1)} %refs_4_.1) | copy-start | bytes 6291460
  47.6 10.9 %copy-start.1 = (f32[8,2048]{1,0:T(8,128)S(1)}, f32[8,2048]{1,0:T(8,128)}, u32[]{:S(2)}) copy-start(f32[8,2048]{1,0:T(8,128)} %first_ref.1) | copy-start | bytes 196612
  47.6 10.9 %copy-start.2 = (f32[8,2048]{1,0:T(8,128)S(1)}, f32[8,2048]{1,0:T(8,128)}, u32[]{:S(2)}) copy-start(f32[8,2048]{1,0:T(8,128)} %second_ref.1) | copy-start | bytes 196612
  50.5 6.6 %collective-permute-start.10 = (bf16[128,512]{1,0:T(8,128)(2,1)S(1)}, bf16[128,512]{1,0:T(8,128)(2,1)S(1)}, u32[]{:S(2)}, u32[]{:S(2)}) collective-permute-start(bf16[128,512]{1,0:T(8,128)(2,1)S(1)} %convolution_convert_fusion.refs_0_), channel_id=1, source_target_pairs={{0,2},{2,0},{1,3},{3,1},{4,6},{6,4},{5,7},{7,5},{8,10},{10,8},{9,1... | collective-permute-start | bytes 393224 | tf_op jit(solution)/shard_map/ppermute | solution.py:30
  52.1 5.0 %collective-permute-start.9 = (bf16[128,512]{1,0:T(8,128)(2,1)S(1)}, bf16[128,512]{1,0:T(8,128)(2,1)S(1)}, u32[]{:S(2)}, u32[]{:S(2)}) collective-permute-start(bf16[128,512]{1,0:T(8,128)(2,1)S(1)} %convolution_convert_fusion.refs_0_), channel_id=1, source_target_pairs={{0,1},{1,0},{2,3},{3,2},{4,5},{5,4},{6,7},{7,6},{8,9},{9,8},{10,11... | collective-permute-start | bytes 393224 | tf_op jit(solution)/shard_map/ppermute | solution.py:30
  57.1 1.3 collective-permute-start.11
  94.6 14.3 %all-to-all-start.2 = ((bf16[8,64,256]{2,1,0:T(8,128)(2,1)}), bf16[8,64,256]{2,1,0:T(8,128)(2,1)S(1)}, u32[]{:S(2)}, u32[]{:S(2)}) async-start(bf16[8,64,256]{2,1,0:T(8,128)(2,1)} %bitcast.24), calls=%async_computation.2 | async-start | bytes 524288 | tf_op jit(solution)/shard_map/all_to_all | solution.py:22
  99.0 14.3 %collective-permute-start.13 = (bf16[1024,128]{1,0:T(8,128)(2,1)S(1)}, bf16[1024,128]{1,0:T(8,128)(2,1)S(1)}, u32[]{:S(2)}, u32[]{:S(2)}) collective-permute-start(bf16[1024,128]{1,0:T(8,128)(2,1)S(1)} %bitcast.45), channel_id=1, source_target_pairs={{0,2},{2,0},{1,3},{3,1},{4,6},{6,4},{5,7},{7,5},{8,10},{10,8},{9,1... | collective-permute-start | bytes 786440 | tf_op jit(solution)/shard_map/ppermute | solution.py:30
  109.7 13.8 %all-to-all-start.3 = ((bf16[8,64,256]{2,1,0:T(8,128)(2,1)}), bf16[8,64,256]{2,1,0:T(8,128)(2,1)S(1)}, u32[]{:S(2)}, u32[]{:S(2)}) async-start(bf16[8,64,256]{2,1,0:T(8,128)(2,1)} %broadcast_in_dim.53), calls=%async_computation.3 | async-start | bytes 524288 | tf_op jit(solution)/shard_map/all_to_all | solution.py:22
  113.1 1.6 %collective-permute-start.12 = (bf16[1024,128]{1,0:T(8,128)(2,1)S(1)}, bf16[1024,128]{1,0:T(8,128)(2,1)S(1)}, u32[]{:S(2)}, u32[]{:S(2)}) collective-permute-start(bf16[1024,128]{1,0:T(8,128)(2,1)S(1)} %bitcast.46), channel_id=1, source_target_pairs={{0,1},{1,0},{2,3},{3,2},{4,5},{5,4},{6,7},{7,6},{8,9},{9,8},{10,11... | collective-permute-start | bytes 786440 | tf_op jit(solution)/shard_map/ppermute | solution.py:30
  113.2 1.9 %collective-permute-start.14 = (bf16[1024,128]{1,0:T(8,128)(2,1)S(1)}, bf16[1024,128]{1,0:T(8,128)(2,1)S(1)}, u32[]{:S(2)}, u32[]{:S(2)}) collective-permute-start(bf16[1024,128]{1,0:T(8,128)(2,1)S(1)} %collective-permute-done.13.refs_2_), channel_id=1, source_target_pairs={{0,1},{1,0},{2,3},{3,2},{4,5},{5,4},{6,7},{7,6},{8,9},{9,8},{10,11... | collective-permute-start | bytes 786440 | tf_op jit(solution)/shard_map/ppermute | solution.py:30

commit v6 on v5

--- a/solution.py
+++ b/solution.py
@@ -13,7 +13,7 @@
 NZ, NX, NYL, NYH, NC = 8, 4, 2, 2, 2
 NP = NX * NYL
 NT = NYH * NC
-PAIR = 2
+PAIR = 4
 MIB = 1024 * 1024
 F32, BF16 = jnp.float32, jnp.bfloat16
 
@@ -156,7 +156,7 @@
 def plane_sums(index, received, own):
     members, rows, part = received.shape
     rank = rows - 4 * own
-    step = rank // 4
+    step = rank // 2
 
     def kernel(index_ref, sums_ref, moments_ref, out, first, second):
         total = sums_ref[0].astype(F32)
@@ -175,7 +175,7 @@
     return call(
         kernel,
         index,
-        (4,),
+        (2,),
         [
             pl.BlockSpec((members, step, part), lambda i, t: (0, i, 0)),
             pl.BlockSpec((members, 4 * own, part), lambda i, t: (0, rank // (4 * own), 0)),

time: 138 us -> 137 us (level)
  no operation moved by 1% of the time
where the time goes in v6:
time: 137 us; the launch traced here: 136 us
  blocking collectives  68 us (50%)
  waiting for transfers between devices  30.3 us (22%)
  starting transfers between devices  23 us (17%)
  Pallas kernels  7.9 us (6%)
  local copies, waits for them, and re-layouts  3.36 us (2%)
  matrix products  2.92 us (2%)
    all_to_all x3, blocking collectives, exchange(): return lax.all_to_all(blocks, axes, 0, 0, tiled=True)  68 us
    all_to_all x2, waiting for transfers between devices, exchange(): return lax.all_to_all(blocks, axes, 0, 0, tiled=True)  17.4 us
    ppermute x6, starting transfers between devices, along(): return lax.ppermute(block, 'x', [(i, (i + shift) % NX) for i in range(NX)])  9.86 us
    ppermute x9, waiting for transfers between devices, swap(): return lax.ppermute(block, axis, ((0, 1), (1, 0)))  9.58 us
    all_to_all x2, starting transfers between devices, exchange(): return lax.all_to_all(blocks, axes, 0, 0, tiled=True)  6.83 us
    ppermute x9, starting transfers between devices, swap(): return lax.ppermute(block, axis, ((0, 1), (1, 0)))  6.33 us
    pallas_call x4, Pallas kernels, call(): pl.pallas_call(kernel, grid_spec=pltpu.PrefetchScalarGridSpec(num_scalar_...  4.51 us
    pallas_call x1, Pallas kernels, loaded(): pl.pallas_call(kernel, in_specs=[pl.BlockSpec(memory_space=pltpu.HBM)] *...  3.39 us
  transfers between devices with their start and end apart: 17, of which 11 were waited for; matrix products, arithmetic and copies ran while one was open for 2% of the time, Pallas kernels for 2%

profile of v6, /device:TPU:16, one launch (start us, length us, event | category | flops | bytes accessed | tf_op | source)
XLA Modules:
  0.0 136.4 jit_solution(4441500257960174115)
XLA Ops:
  0.6 0.8 reshape.34
  1.5 23.5 %all_to_all.25 = bf16[32,32,128]{2,1,0:T(8,128)(2,1)S(1)} all-to-all(bf16[32,32,128]{2,1,0:T(8,128)(2,1)S(1)} %bitcast.54), channel_id=1, replica_groups=mesh['z'=8,'x'=4,'yl'=2,'yh'=2,'core'=2] {'z','yh','core'}, dimensions={0} | all-to-all | bytes 524288 | tf_op jit(solution)/shard_map/all_to_all | solution.py:22
  24.9 1.5 %collective-permute-start.1 = (bf16[8,128,128]{2,1,0:T(8,128)(2,1)S(1)}, bf16[8,128,128]{2,1,0:T(8,128)(2,1)S(1)}, u32[]{:S(2)}, u32[]{:S(2)}) collective-permute-start(bf16[8,128,128]{2,1,0:T(8,128)(2,1)S(1)} %bitcast.50), channel_id=1, source_target_pairs={{0,8},{8,16},{16,24},{24,0},{1,9},{9,17},{17,25},{25,1},{2,10},{10... | collective-permute-start | bytes 786440 | tf_op jit(solution)/shard_map/ppermute | solution.py:60
  26.4 1.7 %collective-permute-start.2 = (bf16[8,128,128]{2,1,0:T(8,128)(2,1)S(1)}, bf16[8,128,128]{2,1,0:T(8,128)(2,1)S(1)}, u32[]{:S(2)}, u32[]{:S(2)}) collective-permute-start(bf16[8,128,128]{2,1,0:T(8,128)(2,1)S(1)} %bitcast.51), channel_id=1, source_target_pairs={{0,24},{8,0},{16,8},{24,16},{1,25},{9,1},{17,9},{25,17},{2,26},{10... | collective-permute-start | bytes 786440 | tf_op jit(solution)/shard_map/ppermute | solution.py:60
  28.2 1.3 collective-permute-start
  29.5 3.4 %shard_map.76 = bf16[512,8192]{1,0:T(8,128)(2,1)S(1)} custom-call(bf16[512,8192]{1,0:T(8,128)(2,1)} %refs_0_), custom_call_target="tpu_custom_call" | custom-call | bytes 16777216 | tf_op jit(solution)/shard_map/pallas_call | solution.py:101
  32.9 0.5 broadcast_in_dim.42
  33.4 0.3 collective-permute-done.1
  33.7 0.4 collective-permute-start.3
  34.0 0.0 collective-permute-done.2
  34.1 3.0 %collective-permute-start.4 = (bf16[4,128,128]{2,1,0:T(8,128)(2,1)S(1)}, bf16[4,128,128]{2,1,0:T(8,128)(2,1)S(1)}, u32[]{:S(2)}, u32[]{:S(2)}) collective-permute-start(bf16[4,128,128]{2,1,0:T(8,128)(2,1)S(1)} %slice.9), channel_id=1, source_target_pairs={{0,24},{8,0},{16,8},{24,16},{1,25},{9,1},{17,9},{25,17},{2,26},{10... | collective-permute-start | bytes 393224 | tf_op jit(solution)/shard_map/ppermute | solution.py:60
  37.1 0.0 collective-permute-done
  37.1 0.0 collective-permute-start.5
  37.1 3.2 %collective-permute-start.6 = (bf16[8,128,128]{2,1,0:T(8,128)(2,1)S(1)}, bf16[8,128,128]{2,1,0:T(8,128)(2,1)S(1)}, u32[]{:S(2)}, u32[]{:S(2)}) collective-permute-start(bf16[8,128,128]{2,1,0:T(8,128)(2,1)S(1)} %collective-permute-done), channel_id=1, source_target_pairs={{0,24},{8,0},{16,8},{24,16},{1,25},{9,1},{17,9},{25,17},{2,26},{10... | collective-permute-start | bytes 786440 | tf_op jit(solution)/shard_map/ppermute | solution.py:60
  40.5 0.7 collective-permute-done.3
  41.1 1.3 collective-permute-start.7
  42.4 0.0 collective-permute-done.4
  42.4 0.7 collective-permute-start.8
  43.2 2.3 %collective-permute-done.5 = bf16[8,128,128]{2,1,0:T(8,128)(2,1)S(1)} collective-permute-done((bf16[8,128,128]{2,1,0:T(8,128)(2,1)S(1)}, bf16[8,128,128]{2,1,0:T(8,128)(2,1)S(1)}, u32[]{:S(2)}, u32[]{:S(2)}) %collective-permute-start.5) | collective-permute-done | bytes 262176 | tf_op jit(solution)/shard_map/ppermute | solution.py:60
  45.6 0.0 collective-permute-done.6
  45.7 0.5 collective-permute-done.7
  46.1 1.4 %collective-permute-done.8 = bf16[4,128,128]{2,1,0:T(8,128)(2,1)S(1)} collective-permute-done((bf16[4,128,128]{2,1,0:T(8,128)(2,1)S(1)}, bf16[4,128,128]{2,1,0:T(8,128)(2,1)S(1)}, u32[]{:S(2)}, u32[]{:S(2)}) %collective-permute-start.8) | collective-permute-done | bytes 131104 | tf_op jit(solution)/shard_map/ppermute | solution.py:30
  47.5 0.0 copy-start.3
  47.5 0.0 copy-start
  47.6 0.0 copy-start.1
  47.6 0.0 copy-start.2
  47.6 2.9 %convolution_convert_fusion.refs_0_ = bf16[128,512]{1,0:T(8,128)(2,1)S(1)} fusion(bf16[8192,128]{1,0:T(8,128)(2,1)S(1)} %bitcast.49, bf16[512,8192]{1,0:T(8,128)(2,1)S(1)} %shard_map.76), kind=kOutput, calls=%fused_computation | convolution fusion | flops 1073807360 | bytes 10616832 | tf_op jit(solution)/shard_map/dot_general | solution.py:116
  50.5 0.0 copy-done.3
  50.5 1.6 %collective-permute-start.10 = (bf16[128,512]{1,0:T(8,128)(2,1)S(1)}, bf16[128,512]{1,0:T(8,128)(2,1)S(1)}, u32[]{:S(2)}, u32[]{:S(2)}) collective-permute-start(bf16[128,512]{1,0:T(8,128)(2,1)S(1)} %convolution_convert_fusion.refs_0_), channel_id=1, source_target_pairs={{0,2},{2,0},{1,3},{3,1},{4,6},{6,4},{5,7},{7,5},{8,10},{10,8},{9,1... | collective-permute-start | bytes 393224 | tf_op jit(solution)/shard_map/ppermute | solution.py:30
  52.1 0.0 collective-permute-start.9
  52.1 5.0 %collective-permute-done.10.refs_2_ = bf16[128,512]{1,0:T(8,128)(2,1)S(1)} collective-permute-done((bf16[128,512]{1,0:T(8,128)(2,1)S(1)}, bf16[128,512]{1,0:T(8,128)(2,1)S(1)}, u32[]{:S(2)}, u32[]{:S(2)}) %collective-permute-start.10) | collective-permute-done | bytes 131104 | tf_op jit(solution)/shard_map/ppermute | solution.py:30
  57.1 0.0 collective-permute-start.11
  57.1 0.0 collective-permute-done.9.refs_1_
  57.1 1.3 collective-permute-done.11.refs_3_
  58.4 0.0 copy-done
  58.4 0.0 copy-done.1
  58.4 0.0 copy-done.2
  58.4 1.6 %shard_map.77 = bf16[8,544,256]{2,1,0:T(8,128)(2,1)S(1)} custom-call(s32[1]{0:T(128)} %bitcast.index_ref, bf16[128,512]{1,0:T(8,128)(2,1)S(1)} %convolution_convert_fusion.refs_0_, bf16[128,512]{1,0:T(8,128)(2,1)S(1)} %collective-permute-done.9.refs_1_, bf16[128,512]{1,0:T(8,128)(2,1)S(1)} %collective-permute-done.10.refs_2_, ...), custom_call_target="tpu_custom_call" | custom-call | flops 1073741824 | bytes 4325376 | tf_op jit(solution)/shard_map/pallas_call | solution.py:44
  60.1 32.4 %all_to_all.26.sums_ref.moments_ref = bf16[8,544,256]{2,1,0:T(8,128)(2,1)S(1)} all-to-all(bf16[8,544,256]{2,1,0:T(8,128)(2,1)S(1)} %shard_map.77), channel_id=1, replica_groups=mesh['z'=8,'x'=4,'yl'=2,'yh'=2,'core'=2] {'x','yl'}, dimensions={0} | all-to-all | bytes 4456448 | tf_op jit(solution)/shard_map/all_to_all | solution.py:22
  92.5 1.2 shard_map.78
  93.7 3.4 %all-to-all-start.2 = ((bf16[8,64,256]{2,1,0:T(8,128)(2,1)}), bf16[8,64,256]{2,1,0:T(8,128)(2,1)S(1)}, u32[]{:S(2)}, u32[]{:S(2)}) async-start(bf16[8,64,256]{2,1,0:T(8,128)(2,1)} %bitcast.24), calls=%async_computation.2 | async-start | bytes 524288 | tf_op jit(solution)/shard_map/all_to_all | solution.py:22
  97.1 1.0 constant_dynamic-slice_fusion
  98.1 0.9 collective-permute-start.13
  98.9 9.0 %all-to-all-done.2 = bf16[8,64,256]{2,1,0:T(8,128)(2,1)S(1)} async-done(((bf16[8,64,256]{2,1,0:T(8,128)(2,1)}), bf16[8,64,256]{2,1,0:T(8,128)(2,1)S(1)}, u32[]{:S(2)}, u32[]{:S(2)}) %all-to-all-start.2) | async-done | bytes 262176 | tf_op jit(solution)/shard_map/all_to_all | solution.py:22
  108.0 0.1 fusion.5
  108.0 0.7 broadcast_in_dim.53
  108.8 3.4 %all-to-all-start.3 = ((bf16[8,64,256]{2,1,0:T(8,128)(2,1)}), bf16[8,64,256]{2,1,0:T(8,128)(2,1)S(1)}, u32[]{:S(2)}, u32[]{:S(2)}) async-start(bf16[8,64,256]{2,1,0:T(8,128)(2,1)} %broadcast_in_dim.53), calls=%async_computation.3 | async-start | bytes 524288 | tf_op jit(solution)/shard_map/all_to_all | solution.py:22
  112.2 0.1 collective-permute-start.12
  112.3 0.0 collective-permute-done.13.refs_2_
  112.3 0.5 collective-permute-start.14
  112.8 1.0 collective-permute-done.12.refs_1_
  113.8 0.4 collective-permute-done.14.refs_3_
  114.2 8.4 %all-to-all-done.3 = bf16[8,64,256]{2,1,0:T(8,128)(2,1)S(1)} async-done(((bf16[8,64,256]{2,1,0:T(8,128)(2,1)}), bf16[8,64,256]{2,1,0:T(8,128)(2,1)S(1)}, u32[]{:S(2)}, u32[]{:S(2)}) %all-to-all-start.3) | async-done | bytes 262176 | tf_op jit(solution)/shard_map/all_to_all | solution.py:22
  122.6 0.9 shard_map.79
  123.4 12.1 %all_to_all.27.back_ref = bf16[8,144,256]{2,1,0:T(8,128)(2,1)S(1)} all-to-all(bf16[8,144,256]{2,1,0:T(8,128)(2,1)S(1)} %shard_map.79), channel_id=1, replica_groups=mesh['z'=8,'x'=4,'yl'=2,'yh'=2,'core'=2] {'x','yl'}, dimensions={0} | all-to-all | bytes 1179648 | tf_op jit(solution)/shard_map/all_to_all | solution.py:22
  135.6 0.8 shard_map.80
  (15 shorter events, 0.4 us)
Async XLA Ops:
  24.9 8.7 %collective-permute-start.1 = (bf16[8,128,128]{2,1,0:T(8,128)(2,1)S(1)}, bf16[8,128,128]{2,1,0:T(8,128)(2,1)S(1)}, u32[]{:S(2)}, u32[]{:S(2)}) collective-permute-start(bf16[8,128,128]{2,1,0:T(8,128)(2,1)S(1)} %bitcast.50), channel_id=1, source_target_pairs={{0,8},{8,16},{16,24},{24,0},{1,9},{9,17},{17,25},{25,1},{2,10},{10... | collective-permute-start | bytes 786440 | tf_op jit(solution)/shard_map/ppermute | solution.py:60
  26.4 7.6 %collective-permute-start.2 = (bf16[8,128,128]{2,1,0:T(8,128)(2,1)S(1)}, bf16[8,128,128]{2,1,0:T(8,128)(2,1)S(1)}, u32[]{:S(2)}, u32[]{:S(2)}) collective-permute-start(bf16[8,128,128]{2,1,0:T(8,128)(2,1)S(1)} %bitcast.51), channel_id=1, source_target_pairs={{0,24},{8,0},{16,8},{24,16},{1,25},{9,1},{17,9},{25,17},{2,26},{10... | collective-permute-start | bytes 786440 | tf_op jit(solution)/shard_map/ppermute | solution.py:60
  28.2 8.9 %collective-permute-start = (bf16[8,128,128]{2,1,0:T(8,128)(2,1)S(1)}, bf16[8,128,128]{2,1,0:T(8,128)(2,1)S(1)}, u32[]{:S(2)}, u32[]{:S(2)}) collective-permute-start(bf16[8,128,128]{2,1,0:T(8,128)(2,1)S(1)} %bitcast.52), channel_id=1, source_target_pairs={{0,4},{4,0},{1,5},{5,1},{2,6},{6,2},{3,7},{7,3},{8,12},{12,8},{9,1... | collective-permute-start | bytes 786440 | tf_op jit(solution)/shard_map/ppermute | solution.py:30
  33.7 7.5 %collective-permute-start.3 = (bf16[4,128,128]{2,1,0:T(8,128)(2,1)S(1)}, bf16[4,128,128]{2,1,0:T(8,128)(2,1)S(1)}, u32[]{:S(2)}, u32[]{:S(2)}) collective-permute-start(bf16[4,128,128]{2,1,0:T(8,128)(2,1)S(1)} %slice.8), channel_id=1, source_target_pairs={{0,8},{8,16},{16,24},{24,0},{1,9},{9,17},{17,25},{25,1},{2,10},{10... | collective-permute-start | bytes 393224 | tf_op jit(solution)/shard_map/ppermute | solution.py:60
  34.1 8.4 %collective-permute-start.4 = (bf16[4,128,128]{2,1,0:T(8,128)(2,1)S(1)}, bf16[4,128,128]{2,1,0:T(8,128)(2,1)S(1)}, u32[]{:S(2)}, u32[]{:S(2)}) collective-permute-start(bf16[4,128,128]{2,1,0:T(8,128)(2,1)S(1)} %slice.9), channel_id=1, source_target_pairs={{0,24},{8,0},{16,8},{24,16},{1,25},{9,1},{17,9},{25,17},{2,26},{10... | collective-permute-start | bytes 393224 | tf_op jit(solution)/shard_map/ppermute | solution.py:60
  37.1 8.5 %collective-permute-start.5 = (bf16[8,128,128]{2,1,0:T(8,128)(2,1)S(1)}, bf16[8,128,128]{2,1,0:T(8,128)(2,1)S(1)}, u32[]{:S(2)}, u32[]{:S(2)}) collective-permute-start(bf16[8,128,128]{2,1,0:T(8,128)(2,1)S(1)} %collective-permute-done), channel_id=1, source_target_pairs={{0,8},{8,16},{16,24},{24,0},{1,9},{9,17},{17,25},{25,1},{2,10},{10... | collective-permute-start | bytes 786440 | tf_op jit(solution)/shard_map/ppermute | solution.py:60
  37.1 8.5 %collective-permute-start.6 = (bf16[8,128,128]{2,1,0:T(8,128)(2,1)S(1)}, bf16[8,128,128]{2,1,0:T(8,128)(2,1)S(1)}, u32[]{:S(2)}, u32[]{:S(2)}) collective-permute-start(bf16[8,128,128]{2,1,0:T(8,128)(2,1)S(1)} %collective-permute-done), channel_id=1, source_target_pairs={{0,24},{8,0},{16,8},{24,16},{1,25},{9,1},{17,9},{25,17},{2,26},{10... | collective-permute-start | bytes 786440 | tf_op jit(solution)/shard_map/ppermute | solution.py:60
  41.1 5.0 %collective-permute-start.7 = (bf16[4,128,128]{2,1,0:T(8,128)(2,1)S(1)}, bf16[4,128,128]{2,1,0:T(8,128)(2,1)S(1)}, u32[]{:S(2)}, u32[]{:S(2)}) collective-permute-start(bf16[4,128,128]{2,1,0:T(8,128)(2,1)S(1)} %collective-permute-done.3), channel_id=1, source_target_pairs={{0,4},{4,0},{1,5},{5,1},{2,6},{6,2},{3,7},{7,3},{8,12},{12,8},{9,1... | collective-permute-start | bytes 393224 | tf_op jit(solution)/shard_map/ppermute | solution.py:30
  42.4 5.1 %collective-permute-start.8 = (bf16[4,128,128]{2,1,0:T(8,128)(2,1)S(1)}, bf16[4,128,128]{2,1,0:T(8,128)(2,1)S(1)}, u32[]{:S(2)}, u32[]{:S(2)}) collective-permute-start(bf16[4,128,128]{2,1,0:T(8,128)(2,1)S(1)} %collective-permute-done.4), channel_id=1, source_target_pairs={{0,4},{4,0},{1,5},{5,1},{2,6},{6,2},{3,7},{7,3},{8,12},{12,8},{9,1... | collective-permute-start | bytes 393224 | tf_op jit(solution)/shard_map/ppermute | solution.py:30
  47.5 3.0 %copy-start.3 = (bf16[8,8,128,128]{3,2,1,0:T(8,128)(2,1)}, bf16[8,8,128,128]{3,2,1,0:T(8,128)(2,1)S(1)}, u32[]{:S(2)}) copy-start(bf16[8,8,128,128]{3,2,1,0:T(8,128)(2,1)S(1)} %bitcast_dynamic-update-slice_fusion.8) | copy-start | bytes 6291460
  47.5 10.9 %copy-start = (bf16[512,2048]{1,0:T(8,128)(2,1)S(1)}, bf16[512,2048]{1,0:T(8,128)(2,1)}, u32[]{:S(2)}) copy-start(bf16[512,2048]{1,0:T(8,128)(2,1)} %refs_4_.1) | copy-start | bytes 6291460
  47.6 10.9 %copy-start.1 = (f32[8,2048]{1,0:T(8,128)S(1)}, f32[8,2048]{1,0:T(8,128)}, u32[]{:S(2)}) copy-start(f32[8,2048]{1,0:T(8,128)} %first_ref.1) | copy-start | bytes 196612
  47.6 10.9 %copy-start.2 = (f32[8,2048]{1,0:T(8,128)S(1)}, f32[8,2048]{1,0:T(8,128)}, u32[]{:S(2)}) copy-start(f32[8,2048]{1,0:T(8,128)} %second_ref.1) | copy-start | bytes 196612
  50.5 6.6 %collective-permute-start.10 = (bf16[128,512]{1,0:T(8,128)(2,1)S(1)}, bf16[128,512]{1,0:T(8,128)(2,1)S(1)}, u32[]{:S(2)}, u32[]{:S(2)}) collective-permute-start(bf16[128,512]{1,0:T(8,128)(2,1)S(1)} %convolution_convert_fusion.refs_0_), channel_id=1, source_target_pairs={{0,2},{2,0},{1,3},{3,1},{4,6},{6,4},{5,7},{7,5},{8,10},{10,8},{9,1... | collective-permute-start | bytes 393224 | tf_op jit(solution)/shard_map/ppermute | solution.py:30
  52.1 5.0 %collective-permute-start.9 = (bf16[128,512]{1,0:T(8,128)(2,1)S(1)}, bf16[128,512]{1,0:T(8,128)(2,1)S(1)}, u32[]{:S(2)}, u32[]{:S(2)}) collective-permute-start(bf16[128,512]{1,0:T(8,128)(2,1)S(1)} %convolution_convert_fusion.refs_0_), channel_id=1, source_target_pairs={{0,1},{1,0},{2,3},{3,2},{4,5},{5,4},{6,7},{7,6},{8,9},{9,8},{10,11... | collective-permute-start | bytes 393224 | tf_op jit(solution)/shard_map/ppermute | solution.py:30
  57.1 1.3 collective-permute-start.11
  93.7 14.3 %all-to-all-start.2 = ((bf16[8,64,256]{2,1,0:T(8,128)(2,1)}), bf16[8,64,256]{2,1,0:T(8,128)(2,1)S(1)}, u32[]{:S(2)}, u32[]{:S(2)}) async-start(bf16[8,64,256]{2,1,0:T(8,128)(2,1)} %bitcast.24), calls=%async_computation.2 | async-start | bytes 524288 | tf_op jit(solution)/shard_map/all_to_all | solution.py:22
  98.1 14.2 %collective-permute-start.13 = (bf16[1024,128]{1,0:T(8,128)(2,1)S(1)}, bf16[1024,128]{1,0:T(8,128)(2,1)S(1)}, u32[]{:S(2)}, u32[]{:S(2)}) collective-permute-start(bf16[1024,128]{1,0:T(8,128)(2,1)S(1)} %bitcast.45), channel_id=1, source_target_pairs={{0,2},{2,0},{1,3},{3,1},{4,6},{6,4},{5,7},{7,5},{8,10},{10,8},{9,1... | collective-permute-start | bytes 786440 | tf_op jit(solution)/shard_map/ppermute | solution.py:30
  108.8 13.8 %all-to-all-start.3 = ((bf16[8,64,256]{2,1,0:T(8,128)(2,1)}), bf16[8,64,256]{2,1,0:T(8,128)(2,1)S(1)}, u32[]{:S(2)}, u32[]{:S(2)}) async-start(bf16[8,64,256]{2,1,0:T(8,128)(2,1)} %broadcast_in_dim.53), calls=%async_computation.3 | async-start | bytes 524288 | tf_op jit(solution)/shard_map/all_to_all | solution.py:22
  112.2 1.6 %collective-permute-start.12 = (bf16[1024,128]{1,0:T(8,128)(2,1)S(1)}, bf16[1024,128]{1,0:T(8,128)(2,1)S(1)}, u32[]{:S(2)}, u32[]{:S(2)}) collective-permute-start(bf16[1024,128]{1,0:T(8,128)(2,1)S(1)} %bitcast.46), channel_id=1, source_target_pairs={{0,1},{1,0},{2,3},{3,2},{4,5},{5,4},{6,7},{7,6},{8,9},{9,8},{10,11... | collective-permute-start | bytes 786440 | tf_op jit(solution)/shard_map/ppermute | solution.py:30
  112.3 1.9 %collective-permute-start.14 = (bf16[1024,128]{1,0:T(8,128)(2,1)S(1)}, bf16[1024,128]{1,0:T(8,128)(2,1)S(1)}, u32[]{:S(2)}, u32[]{:S(2)}) collective-permute-start(bf16[1024,128]{1,0:T(8,128)(2,1)S(1)} %collective-permute-done.13.refs_2_), channel_id=1, source_target_pairs={{0,1},{1,0},{2,3},{3,2},{4,5},{5,4},{6,7},{7,6},{8,9},{9,8},{10,11... | collective-permute-start | bytes 786440 | tf_op jit(solution)/shard_map/ppermute | solution.py:30
